TPU v7x, 32 devices: a whole 2x2x4 slice. The times are simulated.
32 devices in a mesh: row: 8 (over z, y), col: 4 (over x, core).
Axes of the slice: x: 2, y: 2, z: 4, core: 2. Of those that a mesh axis runs over, the one named last changes fastest.
Arguments:
- activations: bfloat16 [8192, 4096], P(('row', 'col')), may hold values from -6 to 6
- out_grads: bfloat16 [8192, 4096], P(('row', 'col')), may hold values from -6 to 6
- proj_in: bfloat16 [4096, 128], replicated, may hold values from -0.09375 to 0.09375
- proj_out: bfloat16 [4096, 128], replicated, may hold values from -0.09375 to 0.09375
- lengths: int32 [256], P(('row', 'col')), may hold values from 1 to 32, 6144 in all
- gram_old: float32 [16384, 16384], P('row', 'col'), as said below
- queries: float32 [16384, 256], P('row'), may hold values from -96 to 96
Outputs:
- gram_new: float32 [16384, 16384], P('row', 'col')
- solution: float32 [16384, 256], P('row')
Inputs may be any that keep to these rules, and one draw needn't show every extreme that they name: `gram_old`: symmetric and positive definite. Example e's token slots from lengths[e] on are padding.
All inputs are finite; a program needn't handle non-finite values. No bound on the sum of `lengths` on one device may be relied on, other than what follows from the above.
Results may differ from a plain program's by a relative error of at most 0.0055.
Values may be sent and summed in bfloat16 or wider, within the bound.
No kernel may reach another device: no remote copies, remote signals or barrier semaphores. Data moves between devices by JAX's collectives and lax.ppermute only.
A program may use at most 192 MiB of HBM per device.

v0:
```python
import functools

import jax
import jax.numpy as jnp
from jax import lax
from jax.experimental import pallas as pl
from jax.experimental.pallas import tpu as pltpu
from jax.sharding import PartitionSpec as P

SEQ = 32

decay_rate = 0.5
damping = 1.0

BF = jnp.bfloat16
F32 = jnp.float32
VMEM_BYTES = 40 * 1024 * 1024


def dot(a, b, dims=((1,), (0,))):
    return lax.dot_general(a, b, (dims, ((), ())), preferred_element_type=F32)


def params(mebibytes=24):
    return pltpu.CompilerParams(vmem_limit_bytes=mebibytes * 1024 * 1024)


def cost(flops, moved):
    return pl.CostEstimate(flops=flops, bytes_accessed=moved, transcendentals=0)


def grads_kernel(parts, outs_col, outs_row, at_ref, *refs):
    own_refs, mate_refs = refs[:parts], refs[parts : 2 * parts]
    col_ref, row_ref, rows_ref, picked_ref = refs[2 * parts :]
    tiers, depth, rank = own_refs[0].shape
    tokens = depth // 2
    slots = tokens // SEQ
    halves = tokens // rank
    outs = outs_col + outs_row
    files = parts // 2
    z, y, x = at_ref[0] // 2, at_ref[0] % 2, at_ref[1] // 2
    even = at_ref[1] % 2 == 0
    example = lax.broadcasted_iota(jnp.int32, (slots, rank), 0)
    token = lax.broadcasted_iota(jnp.int32, (slots, rank), 1)
    masks = [((token + h * rank) // SEQ == example).astype(F32) for h in range(halves)]
    col_at = pl.multiple_of(at_ref[1] * outs_col, outs_col)
    row_at = pl.multiple_of(at_ref[0] * outs_row, outs_row)

    def build(k, low_in):
        left = []
        for h in range(halves):
            picked_ref[k, h, :outs_col, :] = rows_ref[k, pl.ds(h * rank + col_at, outs_col), :]
            picked_ref[k, h, outs_col:, :] = rows_ref[k, pl.ds(h * rank + row_at, outs_row), :]
        for h in range(halves):
            rows = picked_ref[k, h]
            spread = rows[:, None, :] * masks[h][None, :, :]
            left.append(spread.reshape(outs * slots, rank).astype(BF))
        left = jnp.concatenate(left, axis=1)
        return dot(left, low_in).reshape(outs, slots, rank)

    for part in range(parts):
        from_x = lax.rem(x - part // 2 + files, files)

        def chunk(i, carry, part=part, from_x=from_x):
            own, mate = own_refs[part][i], mate_refs[part][i]
            rows_ref[0] = jnp.where(even, own[tokens:, :], mate[tokens:, :]).astype(F32)
            rows_ref[1] = jnp.where(even, mate[tokens:, :], own[tokens:, :]).astype(F32)
            first = jnp.where(even, own[:tokens, :], mate[:tokens, :])
            second = jnp.where(even, mate[:tokens, :], own[:tokens, :])
            both = jnp.concatenate([build(0, first), build(1, second)], axis=1).astype(BF)
            from_z = lax.rem(z - i + tiers, tiers)
            place = ((from_x * tiers + from_z) * 2 + (y ^ (part % 2))) * (2 * slots)
            place = pl.ds(pl.multiple_of(place, 2 * slots), 2 * slots)
            for o in range(outs_col):
                col_ref[place, o * rank : (o + 1) * rank] = both[o]
            for o in range(outs_row):
                row_ref[place, o * rank : (o + 1) * rank] = both[outs_col + o]
            return carry

        lax.fori_loop(0, tiers, chunk, 0)


def build_grads(place, own, mate, rows, cols):
    parts = len(own)
    tiers, depth, rank = own[0].shape
    tokens = depth // 2
    total = 2 * parts * tiers * tokens // SEQ
    return pl.pallas_call(
        functools.partial(grads_kernel, parts, cols // rank, rows // rank),
        in_specs=[pl.BlockSpec(memory_space=pltpu.SMEM)]
        + [pl.BlockSpec(memory_space=pltpu.VMEM)] * (2 * parts),
        out_specs=[pl.BlockSpec(memory_space=pltpu.VMEM)] * 2,
        out_shape=[
            jax.ShapeDtypeStruct((total, cols), BF),
            jax.ShapeDtypeStruct((total, rows), BF),
        ],
        scratch_shapes=[
            pltpu.VMEM((2, tokens, rank), F32),
            pltpu.VMEM((2, tokens // rank, (cols + rows) // rank, rank), F32),
        ],
        compiler_params=params(16),
        cost_estimate=cost(2 * total * (rows + cols) * tokens, 2 * total * (rows + cols)),
        name="build_grads",
    )(place, *own, *mate)


def back_kernel(streams, plan_ref, *refs):
    vec_ref, gram_refs, out_ref = refs[0], refs[1 : 1 + streams], refs[-1]
    depth = gram_refs[0].shape[0]
    total = None
    for s in range(streams):
        vec = vec_ref[:, s * depth : (s + 1) * depth]
        value = dot(vec, gram_refs[s][...].astype(BF))
        total = value if total is None else total + value
    total = decay_rate * total.T
    if len(refs) > streams + 2:
        own = jnp.where(plan_ref[1] == 1, damping, 0.0)
        total = total + own * refs[streams + 1][...]
    out_ref[...] = total.astype(out_ref.dtype)


def back_product(plan, vec, gram, queries=None):
    count, rows = vec.shape
    width = gram.shape[1] // 2
    block = min(512, width)
    steps = width // block
    streams = 2
    depth = rows // streams

    def gram_at(s, i, plan_ref):
        return (s, plan_ref[0] * steps + i)

    in_specs = [pl.BlockSpec((count, rows), lambda i, plan_ref: (0, 0))]
    for s in range(streams):
        in_specs.append(pl.BlockSpec((depth, block), functools.partial(gram_at, s)))
    args = [vec] + [gram] * streams
    kind = BF
    if queries is not None:
        in_specs.append(pl.BlockSpec((block, count), lambda i, plan_ref: (i, 0)))
        args.append(queries)
        kind = F32
    return pl.pallas_call(
        functools.partial(back_kernel, streams),
        grid_spec=pltpu.PrefetchScalarGridSpec(
            num_scalar_prefetch=1,
            grid=(steps,),
            in_specs=in_specs,
            out_specs=pl.BlockSpec((block, count), lambda i, plan_ref: (i, 0)),
        ),
        out_shape=jax.ShapeDtypeStruct((width, count), kind),
        compiler_params=params(),
        cost_estimate=cost(2 * rows * width * count, 4 * rows * width + 4 * width * count),
        name="back_product",
    )(plan, *args)


def gram_kernel(scale, block, first, at_ref, gram_ref, left_ref, right_ref, *rest):
    out_ref, copy_ref = rest[-2:]
    strip = copy_ref.shape[1] // 3
    lower = ((first + pl.program_id(0)) * block >= strip).astype(jnp.int32)
    left = left_ref[...]
    offset = at_ref[0] + (first + pl.program_id(0)) * block
    ahead = lax.broadcasted_iota(jnp.int32, (block, strip), 0)
    ahead = ahead - lax.broadcasted_iota(jnp.int32, (block, strip), 1)
    for s in range(gram_ref.shape[1] // strip):
        part = slice(s * strip, (s + 1) * strip)
        product = dot(left, right_ref[:, part], ((0,), (0,)))
        value = decay_rate * gram_ref[:, part] + scale * product
        value = value + jnp.where(ahead == s * strip - offset, damping, 0.0)
        out_ref[:, part] = value
        short = value.astype(BF)
        for k in range(3):

            @pl.when(at_ref[1 + 3 * lower + k] == s)
            def _(k=k, short=short):
                copy_ref[:, k * strip : (k + 1) * strip] = short


def update_gram(at, gram, left, right, scale, first, count, block, before):
    rows, cols = gram.shape
    examples = left.shape[0]
    width = 3 * (cols // 4)
    in_specs = [
        pl.BlockSpec((block, cols), lambda i, at_ref: (first + i, 0)),
        pl.BlockSpec((examples, block), lambda i, at_ref: (0, first + i)),
        pl.BlockSpec((examples, cols), lambda i, at_ref: (0, 0)),
    ]
    args = [gram, left, right]
    alias = {}
    if before is not None:
        in_specs.append(pl.BlockSpec(memory_space=pl.ANY))
        args.append(before)
        alias = {4: 0}
    return pl.pallas_call(
        functools.partial(gram_kernel, scale, block, first),
        grid_spec=pltpu.PrefetchScalarGridSpec(
            num_scalar_prefetch=1,
            grid=(count,),
            in_specs=in_specs,
            out_specs=[
                pl.BlockSpec((block, cols), lambda i, at_ref: (first + i, 0)),
                pl.BlockSpec((block, width), lambda i, at_ref: (i, 0)),
            ],
        ),
        out_shape=[
            jax.ShapeDtypeStruct((rows, cols), F32),
            jax.ShapeDtypeStruct((count * block, width), BF),
        ],
        input_output_aliases=alias,
        compiler_params=params(30),
        cost_estimate=cost(2 * count * block * cols * examples, 8 * count * block * cols),
        name="update_gram",
    )(at, *args)


def tail_kernel(scale, even, pieces, plan_ref, *refs):
    same_ref, other_ref, mate_ref, came_ref, rest_ref = refs[:5]
    tiers, piece, count = same_ref.shape
    depth = tiers * piece
    width = depth // 2
    col_ref, row_ref, query_ref = refs[5:8]
    copy_refs, inner_refs = refs[8 : 8 + pieces], refs[8 + pieces : 8 + pieces + tiers]
    mapped_ref, total_ref, vec_same_ref, vec_other_ref, sums_ref = refs[8 + pieces + tiers :]
    inner = sum(ref[...].astype(F32) for ref in reversed(inner_refs))
    inner = (scale * inner).astype(BF)
    tier, y = plan_ref[0], plan_ref[1]
    near, source = plan_ref[6] == 1, plan_ref[7] == 1
    along, square = jnp.zeros((8, count), F32), jnp.zeros((8, count), F32)
    norm = jnp.zeros((8, count), F32)

    def fold(value):
        return jnp.sum(value.reshape(value.shape[0] // 8, 8, count), axis=0)

    def low_rank(ref, start):
        part = ref[:, pl.ds(pl.multiple_of(start * piece, piece), piece)]
        return dot(part, inner, ((0,), (0,)))

    for s in range(tiers):
        quarter = lax.rem(tier - s + tiers, tiers)
        rows = pl.ds(pl.multiple_of(quarter * piece, piece), piece)
        own = same_ref[s].astype(F32)
        value = own + low_rank(col_ref, y * tiers + quarter)
        vec_same_ref[rows, :] = value.astype(BF)
        value = other_ref[s].astype(F32) + low_rank(col_ref, (1 - y) * tiers + quarter)
        vec_other_ref[rows, :] = value.astype(BF)
        here = plan_ref[8] == s // (tiers // 2)
        got = jnp.where(here, came_ref[s % (tiers // 2)], rest_ref[s % (tiers // 2)]).astype(F32)
        got = jnp.where(near, jnp.where(source, own, mate_ref[s].astype(F32)), got)
        value = got + low_rank(row_ref, quarter)
        mapped_ref[rows, :] = value
        query = query_ref[rows, :]
        norm += fold(query * query)
        along += fold(query * value)
        square += fold(value * value)

    def take(ref, quadrant):
        return ref[pl.ds(pl.multiple_of(quadrant * width, width), width), :]

    sums_ref[0] = even * norm
    sums_ref[1] = even * along
    sums_ref[2] = even * square
    sums_ref[3] = jnp.zeros_like(norm)
    weight = plan_ref[4].astype(F32)
    cuts = [(k, h) for k in range(pieces) for h in range(tiers // pieces)]

    def left(k, h):
        start = (k * (tiers // pieces) + h) * piece
        return mapped_ref[start : start + piece, :]

    for k, h in cuts:
        upper = (k * (tiers // pieces) + h) * 2 // tiers
        rows = slice(h * piece, (h + 1) * piece)
        total = weight * dot(copy_refs[k][rows, :width], take(vec_same_ref, upper ^ plan_ref[2]))
        total += 2.0 * dot(
            copy_refs[k][rows, width : 2 * width], take(vec_other_ref, upper ^ plan_ref[3])
        )
        sums_ref[3] += fold(total * left(k, h))

    @pl.when(plan_ref[5] == 1)
    def _():
        for k, h in cuts[: len(cuts) // 2]:
            rows = slice(h * piece, (h + 1) * piece)
            total = 2.0 * dot(copy_refs[k][rows, 2 * width :], vec_same_ref[width:, :])
            sums_ref[3] += fold(total * left(k, h))

    total_ref[...] = jnp.sum(sums_ref[...], axis=1)


def tail(plan, same, other, found, grads_col, grads_row, inner, queries, copies, scale, even):
    rows, count = queries.shape
    args = [same, other, *found, grads_col, grads_row, queries, *copies, *inner]
    return pl.pallas_call(
        functools.partial(tail_kernel, scale, even, len(copies)),
        in_specs=[pl.BlockSpec(memory_space=pltpu.SMEM)]
        + [pl.BlockSpec(memory_space=pltpu.VMEM)] * len(args),
        out_specs=[pl.BlockSpec(memory_space=pltpu.VMEM)] * 2,
        out_shape=[
            jax.ShapeDtypeStruct((rows, count), F32),
            jax.ShapeDtypeStruct((4, count), F32),
        ],
        scratch_shapes=[
            pltpu.VMEM((rows, count), BF),
            pltpu.VMEM((rows, count), BF),
            pltpu.VMEM((4, 8, count), F32),
        ],
        compiler_params=params(16),
        cost_estimate=cost(4 * rows * rows * count, 4 * rows * rows),
        name="tail",
    )(plan, *args)


def after(value, *others):
    return lax.optimization_barrier((value,) + others)[0]


def integers(*values):
    return jnp.stack([jnp.asarray(v).astype(jnp.int32) for v in values])


def shards(activations, out_grads, proj_in, proj_out, lengths, gram_old, queries):
    local_count = lengths.shape[0]
    rank = proj_in.shape[1]
    row_count = lax.axis_size("row")
    col_count = lax.axis_size("col")
    rows, cols = gram_old.shape
    count = queries.shape[1]
    tokens = local_count * SEQ
    tiers = row_count // 2
    files = col_count // 2
    piece = rows // tiers
    row = lax.axis_index("row")
    col = lax.axis_index("col")
    z, y = row // 2, row % 2
    x, core = col // 2, col % 2
    total_examples = local_count * row_count * col_count
    scale = (1.0 - decay_rate) / total_examples

    def move(value, goes):
        pairs = []
        for r in range(row_count):
            for c in range(col_count):
                to = goes(r // 2, r % 2, c // 2, c % 2)
                if to is not None:
                    pairs.append((r * col_count + c, (to[0] * 2 + to[1]) * col_count + to[2] * 2 + to[3]))
        return lax.ppermute(value, ("row", "col"), pairs)

    def swap_y(value):
        return move(value, lambda z, y, x, k: (z, 1 - y, x, k))

    def swap_core(value):
        return move(value, lambda z, y, x, k: (z, y, x, 1 - k))

    def ring_z(value, by=1):
        return move(value, lambda z, y, x, k: ((z + by) % tiers, y, x, k))

    def ring_x(value):
        return move(value, lambda z, y, x, k: (z, y, (x + 1) % files, k))

    def flip_x(value, bit):
        return move(value, lambda z, y, x, k: (z, y, x ^ bit, k))

    def spread_z(value):
        return [value] + [ring_z(value, by) for by in range(1, tiers)]

    vec = queries.astype(BF).T
    away = back_product(integers(1 - y, 0), vec, gram_old)
    come = swap_y(away)

    low_in = dot(activations, proj_in).astype(BF)
    low_out = dot(proj_out, out_grads, ((0,), (1,))).astype(BF)
    slot = jnp.arange(tokens, dtype=jnp.int32)
    valid_mask = slot % SEQ < jnp.repeat(lengths, SEQ)
    low_out = jnp.where(valid_mask[None, :], low_out, jnp.zeros((), BF))
    low_out = low_out.reshape(rank, tokens // rank, rank).transpose(1, 0, 2).reshape(tokens, rank)
    local = after(jnp.concatenate([low_in, low_out], axis=0), away)
    factors = spread_z(local)

    here = back_product(after(integers(y, z == col), local), vec, gram_old, queries)
    here = here.reshape(tiers, piece, count)
    come = come.reshape(tiers, piece, count)

    def piece_for(by):
        at = (z + by) % tiers
        one = lax.dynamic_index_in_dim(here, at, 0, keepdims=False)
        two = lax.dynamic_index_in_dim(come, at, 0, keepdims=False)
        return one + two.astype(F32)

    sends = [piece_for(by).astype(BF) for by in range(1, tiers)]
    parts = [ring_z(sends[by - 1], by) for by in range(1, tiers)]

    factors = jnp.stack(lax.optimization_barrier((*factors, here))[:tiers])
    across = [factors]
    for dx in range(1, files):
        across.append(move(factors, lambda z, y, x, k: (z, y, (x + dx) % files, k)))
    own = []
    for one in across:
        own.append(one)
        own.append(swap_y(after(one, *sends)))

    total = piece_for(0)
    for part in parts:
        total = total + part.astype(F32)
    short = total.astype(BF)

    same = spread_z(short)
    held = lax.optimization_barrier((*own, short))[:-1]
    mate = [swap_core(f) for f in held]
    grads_col, grads_row = build_grads(integers(row, col), held, mate, rows, cols)
    partial = dot(grads_row, queries.astype(BF))
    fetched = swap_y(partial.astype(BF))
    same = lax.optimization_barrier((*same, fetched, partial))[:-1]
    fetched = same[-1]
    stacked = jnp.stack(same[:-1])
    inner = (partial + fetched.astype(F32)).astype(BF)
    sums = spread_z(inner)
    other = swap_y(stacked)

    fellow = swap_core(stacked)
    cut = tiers // 2
    half = lax.dynamic_slice_in_dim(
        jnp.where(core == z % 2, stacked, fellow), core * cut, cut, 0
    )
    found = [fellow]
    for flip in range(2):
        came = half
        for dx in range(1, files):
            got = move(half, lambda z, y, x, k: (z, y, (x + dx) % files, k ^ flip))
            came = got if files == 2 else jnp.where((x - dx) % files == z // 2, got, came)
        found.append(came)

    flags = integers(row > 2 * col + y, row > 2 * col + 1 - y)
    block = min(256, rows // 4)
    at = integers(
        row * rows - col * cols,
        2 * y + flags[0],
        2 * (1 - y) + flags[1],
        jnp.where(z == col, 2 * y + 1, -1),
        2 * y + 1 - flags[0],
        2 * (1 - y) + 1 - flags[1],
        -1,
    )
    gram_new, copy = update_gram(
        after(at, half), gram_old, grads_row, grads_col, scale, 0, rows // block, block, None
    )
    held = lax.optimization_barrier((*found[1:], *sums, gram_new))
    found, sums = [fellow, *held[:2]], held[2:-1]
    plan = jnp.concatenate(
        [
            integers(z, y),
            flags,
            integers(jnp.where(z == col, 1, 2), z == col, x == z // 2, core == z % 2, core),
        ]
    )
    mapped, sums = tail(
        after(plan, gram_new), stacked, other, found, grads_col, grads_row, sums, queries,
        [copy], scale, 1.0 / col_count,
    )
    sums = sums + swap_core(sums)
    bit = 1
    while bit < files:
        sums = sums + flip_x(sums, bit)
        bit *= 2
    sums = sums + swap_y(sums)
    around = jnp.stack(spread_z(sums))
    sums = sum(
        lax.dynamic_index_in_dim(around, (z - k) % tiers, 0, keepdims=False) for k in range(tiers)
    )
    norm_now, along, square, curve = sums[0], sums[1], sums[2], sums[3]
    step = norm_now / along
    norm_next = step * step * square - norm_now
    momentum = norm_next / norm_now
    curvature = along - 2.0 * step * square + step * step * curve
    step_next = norm_next / (curvature - momentum * norm_next / step)
    solution = (step + step_next * (1.0 + momentum)) * queries - (step_next * step) * mapped
    return (gram_new, solution)


def solution(mesh):
    in_specs = (
        P(("row", "col"), None),
        P(("row", "col"), None),
        P(),
        P(),
        P(("row", "col")),
        P("row", "col"),
        P("row", None),
    )
    out_specs = (P("row", "col"), P("row", None))
    return jax.shard_map(shards, mesh=mesh, in_specs=in_specs, out_specs=out_specs, check_vma=False)
```

profile of v0, /device:TPU:0, one launch (start us, length us, event | category | flops | bytes accessed | tf_op | source)
XLA Modules:
  0.0 168.9 jit_solution(4949187057447797515)
XLA Ops:
  0.7 1.9 %copy.10 = bf16[2048,256]{0,1:T(8,128)(2,1)S(1)} copy(f32[2048,256]{1,0:T(8,128)} %refs_7_.1) | data formatting | bytes 3145728 | tf_op args[6]
  2.7 9.1 %back_product.2 = bf16[2048,256]{1,0:T(8,128)(2,1)} custom-call(s32[2]{0:T(128)S(1)} %get-tuple-element.74.plan_ref, bf16[256,2048]{1,0:T(8,128)(2,1)S(1)} %bitcast.105, f32[2048,4096]{1,0:T(8,128)} %gram_ref.1, f32[2048,4096]{1,0:T(8,128)} %gram_ref.1), custom_call_target="tpu_custom_call" | custom-call | flops 2147483648 | bytes 18874368 | tf_op jit(solution)/shard_map/back_product/pallas_call | solution.py:142
  11.7 3.0 %collective-permute-start = (bf16[2048,256]{1,0:T(8,128)(2,1)}, bf16[2048,256]{1,0:T(8,128)(2,1)}, u32[]{:S(2)}, u32[]{:S(2)}) collective-permute-start(bf16[2048,256]{1,0:T(8,128)(2,1)} %back_product.2), channel_id=1, source_target_pairs={{0,4},{1,5},{2,6},{3,7},{4,0},{5,1},{6,2},{7,3},{8,12},{9,13},{10,... | collective-permute-start | bytes 3145736 | tf_op jit(solution)/shard_map/ppermute | solution.py:345
  14.9 2.2 %fusion.1 = bf16[16,2,8,128]{3,2,1,0:T(8,128)(2,1)S(1)} fusion(bf16[4096,128]{1,0:T(8,128)(2,1)} %param.10, bf16[256,4096]{1,0:T(8,128)(2,1)S(1)} %copy-done, pred[256]{0:T(512)(128)(4,1)S(1)} %fusion.10), kind=kOutput, calls=%fused_computation.4 | convolution fusion | flops 268500992 | bytes 3211520 | tf_op jit(solution)/shard_map/dot_general | solution.py:21
  17.9 1.6 collective-permute-start.7
  19.5 2.6 %collective-permute-start.8 = (bf16[512,128]{1,0:T(8,128)(2,1)S(1)}, bf16[512,128]{1,0:T(8,128)(2,1)S(1)}, u32[]{:S(2)}, u32[]{:S(2)}) collective-permute-start(bf16[512,128]{1,0:T(8,128)(2,1)S(1)} %pad_maximum_fusion.2), channel_id=1, source_target_pairs={{0,16},{1,17},{2,18},{3,19},{4,20},{5,21},{6,22},{7,23},{8,24},{9,... | collective-permute-start | bytes 393224 | tf_op jit(solution)/shard_map/ppermute | solution.py:345
  22.1 1.3 collective-permute-start.9
  23.4 8.2 %back_product.3 = f32[2048,256]{1,0:T(8,128)S(1)} custom-call(s32[2]{0:T(128)S(1)} %get-tuple-element.34.plan_ref, bf16[256,2048]{1,0:T(8,128)(2,1)S(1)} %bitcast.106, f32[2048,4096]{1,0:T(8,128)} %gram_ref.1, f32[2048,4096]{1,0:T(8,128)} %gram_ref.1, f32[2048,256]{1,0:T(8,128)S(1)} %copy-done.2), custom_call_target="tpu_custom_call" | custom-call | flops 2147483648 | bytes 18874368 | tf_op jit(solution)/shard_map/back_product/pallas_call | solution.py:142
  32.6 1.5 collective-permute-start.11
  34.0 4.1 %collective-permute-done = bf16[2048,256]{1,0:T(8,128)(2,1)} collective-permute-done((bf16[2048,256]{1,0:T(8,128)(2,1)}, bf16[2048,256]{1,0:T(8,128)(2,1)}, u32[]{:S(2)}, u32[]{:S(2)}) %collective-permute-start) | collective-permute-done | bytes 1048608 | tf_op jit(solution)/shard_map/ppermute | solution.py:345
  38.2 2.1 %fusion.7 = (bf16[512,256]{1,0:T(8,128)(2,1)}, bf16[512,256]{1,0:T(8,128)(2,1)S(1)}, bf16[512,256]{1,0:T(8,128)(2,1)}) fusion(f32[4,512,256]{2,1,0:T(8,128)S(1)} %bitcast.107, s32[]{:T(128)S(6)} %select_n.130, bf16[4,512,256]{2,1,0:T(8,128)(2,1)} %bitcast.13, s32[]{:T(128)S(6)} %select_n.134, s32[]{:T(128)S(6)} %select_n.132), kind=kLoop, calls=%fused_computation.18 | loop fusion | flops 1179648 | bytes 3145740 | tf_op jit(solution)/shard_map/convert_element_type | solution.py:388
  40.3 5.2 %collective-permute-done.11.refs_2_ = bf16[4,512,128]{2,1,0:T(8,128)(2,1)} collective-permute-done((bf16[4,512,128]{2,1,0:T(8,128)(2,1)}, bf16[4,512,128]{2,1,0:T(8,128)(2,1)}, u32[]{:S(2)}, u32[]{:S(2)}) %collective-permute-start.11) | collective-permute-done | bytes 524320 | tf_op jit(solution)/shard_map/ppermute | solution.py:345
  45.9 1.5 collective-permute-start.10
  47.5 3.5 %collective-permute-start.1 = (bf16[512,256]{1,0:T(8,128)(2,1)}, bf16[512,256]{1,0:T(8,128)(2,1)}, u32[]{:S(2)}, u32[]{:S(2)}) collective-permute-start(bf16[512,256]{1,0:T(8,128)(2,1)} %get-tuple-element.68), channel_id=1, source_target_pairs={{0,8},{1,9},{2,10},{3,11},{4,12},{5,13},{6,14},{7,15},{8,16},{9,17... | collective-permute-start | bytes 786440 | tf_op jit(solution)/shard_map/ppermute | solution.py:345
  50.9 2.4 %collective-permute-start.3 = (bf16[512,256]{1,0:T(8,128)(2,1)S(1)}, bf16[512,256]{1,0:T(8,128)(2,1)}, u32[]{:S(2)}, u32[]{:S(2)}) collective-permute-start(bf16[512,256]{1,0:T(8,128)(2,1)S(1)} %get-tuple-element.69), channel_id=1, source_target_pairs={{0,24},{1,25},{2,26},{3,27},{4,28},{5,29},{6,30},{7,31},{8,0},{9,1... | collective-permute-start | bytes 786440 | tf_op jit(solution)/shard_map/ppermute | solution.py:345
  53.3 5.5 %collective-permute-done.1 = bf16[512,256]{1,0:T(8,128)(2,1)} collective-permute-done((bf16[512,256]{1,0:T(8,128)(2,1)}, bf16[512,256]{1,0:T(8,128)(2,1)}, u32[]{:S(2)}, u32[]{:S(2)}) %collective-permute-start.1) | collective-permute-done | bytes 262176 | tf_op jit(solution)/shard_map/ppermute | solution.py:345
  58.8 8.2 %collective-permute-done.2 = bf16[512,256]{1,0:T(8,128)(2,1)} collective-permute-done((bf16[512,256]{1,0:T(8,128)(2,1)}, bf16[512,256]{1,0:T(8,128)(2,1)}, u32[]{:S(2)}, u32[]{:S(2)}) %collective-permute-start.2) | collective-permute-done | bytes 262176 | tf_op jit(solution)/shard_map/ppermute | solution.py:345
  69.7 5.9 %collective-permute-start.4 = (bf16[512,256]{1,0:T(8,128)(2,1)S(1)}, bf16[512,256]{1,0:T(8,128)(2,1)S(1)}, u32[]{:S(2)}, u32[]{:S(2)}) collective-permute-start(bf16[512,256]{1,0:T(8,128)(2,1)S(1)} %fusion.4), channel_id=1, source_target_pairs={{0,8},{1,9},{2,10},{3,11},{4,12},{5,13},{6,14},{7,15},{8,16},{9,17... | collective-permute-start | bytes 786440 | tf_op jit(solution)/shard_map/ppermute | solution.py:345
  75.7 3.1 %collective-permute-start.5 = (bf16[512,256]{1,0:T(8,128)(2,1)S(1)}, bf16[512,256]{1,0:T(8,128)(2,1)S(1)}, u32[]{:S(2)}, u32[]{:S(2)}) collective-permute-start(bf16[512,256]{1,0:T(8,128)(2,1)S(1)} %fusion.4), channel_id=1, source_target_pairs={{0,16},{1,17},{2,18},{3,19},{4,20},{5,21},{6,22},{7,23},{8,24},{9,... | collective-permute-start | bytes 786440 | tf_op jit(solution)/shard_map/ppermute | solution.py:345
  80.0 6.4 %build_grads.1 = (bf16[256,4096]{1,0:T(8,128)(2,1)S(1)}, bf16[256,2048]{1,0:T(8,128)(2,1)S(1)}) custom-call(s32[2]{0:T(128)S(1)} %pad_add_fusion.2.at_ref, bf16[4,512,128]{2,1,0:T(8,128)(2,1)} %pad_maximum_fusion.1.refs_0_, bf16[4,512,128]{2,1,0:T(8,128)(2,1)} %collective-permute-done.10.refs_1_, bf16[4,512,128]{2,1,0:T(8,128)(2,1)} %collective-permute-done.11.refs_2_, ...), custom_call_target="tpu_custom_call" | custom-call | flops 805306368 | bytes 3145728 | tf_op jit(solution)/shard_map/build_grads/pallas_call | solution.py:88
  87.4 8.7 %collective-permute-done.5 = bf16[512,256]{1,0:T(8,128)(2,1)S(1)} collective-permute-done((bf16[512,256]{1,0:T(8,128)(2,1)S(1)}, bf16[512,256]{1,0:T(8,128)(2,1)S(1)}, u32[]{:S(2)}, u32[]{:S(2)}) %collective-permute-start.5) | collective-permute-done | bytes 262176 | tf_op jit(solution)/shard_map/ppermute | solution.py:345
  99.3 6.1 %collective-permute-start.22 = (bf16[256,256]{1,0:T(8,128)(2,1)S(1)}, bf16[256,256]{1,0:T(8,128)(2,1)S(1)}, u32[]{:S(2)}, u32[]{:S(2)}) collective-permute-start(bf16[256,256]{1,0:T(8,128)(2,1)S(1)} %add_convert_fusion.3.refs_9_), channel_id=1, source_target_pairs={{0,8},{1,9},{2,10},{3,11},{4,12},{5,13},{6,14},{7,15},{8,16},{9,17... | collective-permute-start | bytes 393224 | tf_op jit(solution)/shard_map/ppermute | solution.py:345
  105.5 2.1 %dynamic-slice_select_fusion = bf16[2,512,256]{2,1,0:T(8,128)(2,1)} fusion(bf16[4,512,256]{2,1,0:T(8,128)(2,1)} %collective-permute-done.18.refs_2_, s32[]{:T(128)S(6)} %select_n.136, bf16[4,512,256]{2,1,0:T(8,128)(2,1)} %pad_maximum_fusion.refs_0_, pred[]{:T(512)S(6)} %eq.29), kind=kLoop, calls=%fused_computation.6 | loop fusion | flops 262144 | bytes 1572869 | tf_op jit(solution)/shard_map/jit(_where)/select_n | solution.py:421
  107.6 1.5 collective-permute-start.20
  109.7 3.4 %collective-permute-start.24 = (bf16[256,256]{1,0:T(8,128)(2,1)S(1)}, bf16[256,256]{1,0:T(8,128)(2,1)S(1)}, u32[]{:S(2)}, u32[]{:S(2)}) collective-permute-start(bf16[256,256]{1,0:T(8,128)(2,1)S(1)} %add_convert_fusion.3.refs_9_), channel_id=1, source_target_pairs={{0,24},{1,25},{2,26},{3,27},{4,28},{5,29},{6,30},{7,31},{8,0},{9,1... | collective-permute-start | bytes 393224 | tf_op jit(solution)/shard_map/ppermute | solution.py:345
  113.1 28.9 %update_gram.1 = (f32[2048,4096]{1,0:T(8,128)}, bf16[2048,3072]{1,0:T(8,128)(2,1)S(1)}) custom-call(s32[7]{0:T(128)S(1)} %stack.128.at_ref, f32[2048,4096]{1,0:T(8,128)} %gram_ref.1, bf16[256,2048]{1,0:T(8,128)(2,1)S(1)} %copy-done.5, bf16[256,4096]{1,0:T(8,128)(2,1)S(1)} %get-tuple-element.51.right_ref.refs_5_), custom_call_target="tpu_custom_call" | custom-call | flops 4294967296 | bytes 67108864 | tf_op jit(solution)/shard_map/update_gram/pallas_call | solution.py:194
  142.1 7.0 %tail.1 = (f32[2048,256]{1,0:T(8,128)S(1)}, f32[4,256]{1,0:T(4,128)S(1)}) custom-call(s32[9]{0:T(128)S(1)} %concatenate.7.plan_ref, bf16[4,512,256]{2,1,0:T(8,128)(2,1)} %pad_maximum_fusion.refs_0_, bf16[4,512,256]{2,1,0:T(8,128)(2,1)} %collective-permute-done.19.refs_1_, bf16[4,512,256]{2,1,0:T(8,128)(2,1)} %collective-permute-done.18.refs_2_, ...), custom_call_target="tpu_custom_call" | custom-call | flops 4294967296 | bytes 16777216 | tf_op jit(solution)/shard_map/tail/pallas_call | solution.py:292
  152.3 2.9 %collective-permute-done.26 = f32[4,256]{1,0:T(4,128)S(1)} collective-permute-done((f32[4,256]{1,0:T(4,128)S(1)}, f32[4,256]{1,0:T(4,128)S(1)}, u32[]{:S(2)}, u32[]{:S(2)}) %collective-permute-start.26) | collective-permute-done | bytes 4128 | tf_op jit(solution)/shard_map/ppermute | solution.py:345
  155.7 3.1 %collective-permute-done.27 = f32[4,256]{1,0:T(4,128)S(1)} collective-permute-done((f32[4,256]{1,0:T(4,128)S(1)}, f32[4,256]{1,0:T(4,128)S(1)}, u32[]{:S(2)}, u32[]{:S(2)}) %collective-permute-start.27) | collective-permute-done | bytes 4128 | tf_op jit(solution)/shard_map/ppermute | solution.py:345
  159.1 3.5 %collective-permute-start.30 = (f32[4,256]{1,0:T(4,128)S(1)}, f32[4,256]{1,0:T(4,128)S(1)}, u32[]{:S(2)}, u32[]{:S(2)}) collective-permute-start(f32[4,256]{1,0:T(4,128)S(1)} %add.209), channel_id=1, source_target_pairs={{0,24},{1,25},{2,26},{3,27},{4,28},{5,29},{6,30},{7,31},{8,0},{9,1... | collective-permute-start | bytes 12296 | tf_op jit(solution)/shard_map/ppermute | solution.py:345
  162.7 1.6 collective-permute-done.28
  164.9 4.0 %multiply_subtract_fusion = f32[2048,256]{1,0:T(8,128)} fusion(f32[2048,256]{1,0:T(8,128)} %copy-done.6, f32[2048,256]{1,0:T(8,128)} %refs_7_.1, f32[256]{0:T(256)S(1)} %bitcast.119, f32[256]{0:T(256)S(1)} %bitcast.120), kind=kLoop, calls=%fused_computation | loop fusion | flops 1572864 | bytes 6293504 | tf_op jit(solution)/shard_map/sub | solution.py:474
  (85 shorter events, 15.7 us)
Async XLA Ops:
  11.7 26.4 %collective-permute-start = (bf16[2048,256]{1,0:T(8,128)(2,1)}, bf16[2048,256]{1,0:T(8,128)(2,1)}, u32[]{:S(2)}, u32[]{:S(2)}) collective-permute-start(bf16[2048,256]{1,0:T(8,128)(2,1)} %back_product.2), channel_id=1, source_target_pairs={{0,4},{1,5},{2,6},{3,7},{4,0},{5,1},{6,2},{7,3},{8,12},{9,13},{10,... | collective-permute-start | bytes 3145736 | tf_op jit(solution)/shard_map/ppermute | solution.py:345
  17.9 13.8 %collective-permute-start.7 = (bf16[512,128]{1,0:T(8,128)(2,1)S(1)}, bf16[512,128]{1,0:T(8,128)(2,1)S(1)}, u32[]{:S(2)}, u32[]{:S(2)}) collective-permute-start(bf16[512,128]{1,0:T(8,128)(2,1)S(1)} %pad_maximum_fusion.2), channel_id=1, source_target_pairs={{0,8},{1,9},{2,10},{3,11},{4,12},{5,13},{6,14},{7,15},{8,16},{9,17... | collective-permute-start | bytes 393224 | tf_op jit(solution)/shard_map/ppermute | solution.py:345
  19.5 12.2 %collective-permute-start.8 = (bf16[512,128]{1,0:T(8,128)(2,1)S(1)}, bf16[512,128]{1,0:T(8,128)(2,1)S(1)}, u32[]{:S(2)}, u32[]{:S(2)}) collective-permute-start(bf16[512,128]{1,0:T(8,128)(2,1)S(1)} %pad_maximum_fusion.2), channel_id=1, source_target_pairs={{0,16},{1,17},{2,18},{3,19},{4,20},{5,21},{6,22},{7,23},{8,24},{9,... | collective-permute-start | bytes 393224 | tf_op jit(solution)/shard_map/ppermute | solution.py:345
  22.1 9.6 %collective-permute-start.9 = (bf16[512,128]{1,0:T(8,128)(2,1)S(1)}, bf16[512,128]{1,0:T(8,128)(2,1)S(1)}, u32[]{:S(2)}, u32[]{:S(2)}) collective-permute-start(bf16[512,128]{1,0:T(8,128)(2,1)S(1)} %pad_maximum_fusion.2), channel_id=1, source_target_pairs={{0,24},{1,25},{2,26},{3,27},{4,28},{5,29},{6,30},{7,31},{8,0},{9,1... | collective-permute-start | bytes 393224 | tf_op jit(solution)/shard_map/ppermute | solution.py:345
  32.6 12.9 %collective-permute-start.11 = (bf16[4,512,128]{2,1,0:T(8,128)(2,1)}, bf16[4,512,128]{2,1,0:T(8,128)(2,1)}, u32[]{:S(2)}, u32[]{:S(2)}) collective-permute-start(bf16[4,512,128]{2,1,0:T(8,128)(2,1)} %pad_maximum_fusion.1.refs_0_), channel_id=1, source_target_pairs={{0,2},{1,3},{2,0},{3,1},{4,6},{5,7},{6,4},{7,5},{8,10},{9,11},{10,... | collective-permute-start | bytes 1572872 | tf_op jit(solution)/shard_map/ppermute | solution.py:345
  45.4 23.0 %collective-permute-start.12 = (bf16[4,512,128]{2,1,0:T(8,128)(2,1)}, bf16[4,512,128]{2,1,0:T(8,128)(2,1)}, u32[]{:S(2)}, u32[]{:S(2)}) collective-permute-start(bf16[4,512,128]{2,1,0:T(8,128)(2,1)} %collective-permute-done.11.refs_2_), channel_id=1, source_target_pairs={{0,4},{1,5},{2,6},{3,7},{4,0},{5,1},{6,2},{7,3},{8,12},{9,13},{10,... | collective-permute-start | bytes 1572872 | tf_op jit(solution)/shard_map/ppermute | solution.py:345
  45.9 22.7 %collective-permute-start.10 = (bf16[4,512,128]{2,1,0:T(8,128)(2,1)}, bf16[4,512,128]{2,1,0:T(8,128)(2,1)}, u32[]{:S(2)}, u32[]{:S(2)}) collective-permute-start(bf16[4,512,128]{2,1,0:T(8,128)(2,1)} %pad_maximum_fusion.1.refs_0_), channel_id=1, source_target_pairs={{0,4},{1,5},{2,6},{3,7},{4,0},{5,1},{6,2},{7,3},{8,12},{9,13},{10,... | collective-permute-start | bytes 1572872 | tf_op jit(solution)/shard_map/ppermute | solution.py:345
  47.5 11.4 %collective-permute-start.1 = (bf16[512,256]{1,0:T(8,128)(2,1)}, bf16[512,256]{1,0:T(8,128)(2,1)}, u32[]{:S(2)}, u32[]{:S(2)}) collective-permute-start(bf16[512,256]{1,0:T(8,128)(2,1)} %get-tuple-element.68), channel_id=1, source_target_pairs={{0,8},{1,9},{2,10},{3,11},{4,12},{5,13},{6,14},{7,15},{8,16},{9,17... | collective-permute-start | bytes 786440 | tf_op jit(solution)/shard_map/ppermute | solution.py:345
  50.9 16.1 %collective-permute-start.2 = (bf16[512,256]{1,0:T(8,128)(2,1)}, bf16[512,256]{1,0:T(8,128)(2,1)}, u32[]{:S(2)}, u32[]{:S(2)}) collective-permute-start(bf16[512,256]{1,0:T(8,128)(2,1)} %get-tuple-element.70), channel_id=1, source_target_pairs={{0,16},{1,17},{2,18},{3,19},{4,20},{5,21},{6,22},{7,23},{8,24},{9,... | collective-permute-start | bytes 786440 | tf_op jit(solution)/shard_map/ppermute | solution.py:345
  50.9 16.1 %collective-permute-start.3 = (bf16[512,256]{1,0:T(8,128)(2,1)S(1)}, bf16[512,256]{1,0:T(8,128)(2,1)}, u32[]{:S(2)}, u32[]{:S(2)}) collective-permute-start(bf16[512,256]{1,0:T(8,128)(2,1)S(1)} %get-tuple-element.69), channel_id=1, source_target_pairs={{0,24},{1,25},{2,26},{3,27},{4,28},{5,29},{6,30},{7,31},{8,0},{9,1... | collective-permute-start | bytes 786440 | tf_op jit(solution)/shard_map/ppermute | solution.py:345
  68.6 7.0 %collective-permute-start.13 = (bf16[4,512,128]{2,1,0:T(8,128)(2,1)}, bf16[4,512,128]{2,1,0:T(8,128)(2,1)S(1)}, u32[]{:S(2)}, u32[]{:S(2)}) collective-permute-start(bf16[4,512,128]{2,1,0:T(8,128)(2,1)} %pad_maximum_fusion.1.refs_0_), channel_id=1, source_target_pairs={{0,1},{1,0},{2,3},{3,2},{4,5},{5,4},{6,7},{7,6},{8,9},{9,8},{10,11... | collective-permute-start | bytes 1572872 | tf_op jit(solution)/shard_map/ppermute | solution.py:345
  68.6 10.1 %collective-permute-start.14 = (bf16[4,512,128]{2,1,0:T(8,128)(2,1)}, bf16[4,512,128]{2,1,0:T(8,128)(2,1)S(1)}, u32[]{:S(2)}, u32[]{:S(2)}) collective-permute-start(bf16[4,512,128]{2,1,0:T(8,128)(2,1)} %collective-permute-done.10.refs_1_), channel_id=1, source_target_pairs={{0,1},{1,0},{2,3},{3,2},{4,5},{5,4},{6,7},{7,6},{8,9},{9,8},{10,11... | collective-permute-start | bytes 1572872 | tf_op jit(solution)/shard_map/ppermute | solution.py:345
  69.1 10.8 %collective-permute-start.15 = (bf16[4,512,128]{2,1,0:T(8,128)(2,1)}, bf16[4,512,128]{2,1,0:T(8,128)(2,1)S(1)}, u32[]{:S(2)}, u32[]{:S(2)}) collective-permute-start(bf16[4,512,128]{2,1,0:T(8,128)(2,1)} %collective-permute-done.11.refs_2_), channel_id=1, source_target_pairs={{0,1},{1,0},{2,3},{3,2},{4,5},{5,4},{6,7},{7,6},{8,9},{9,8},{10,11... | collective-permute-start | bytes 1572872 | tf_op jit(solution)/shard_map/ppermute | solution.py:345
  69.1 10.8 %collective-permute-start.16 = (bf16[4,512,128]{2,1,0:T(8,128)(2,1)}, bf16[4,512,128]{2,1,0:T(8,128)(2,1)S(1)}, u32[]{:S(2)}, u32[]{:S(2)}) collective-permute-start(bf16[4,512,128]{2,1,0:T(8,128)(2,1)} %collective-permute-done.12.refs_3_), channel_id=1, source_target_pairs={{0,1},{1,0},{2,3},{3,2},{4,5},{5,4},{6,7},{7,6},{8,9},{9,8},{10,11... | collective-permute-start | bytes 1572872 | tf_op jit(solution)/shard_map/ppermute | solution.py:345
  69.7 17.7 %collective-permute-start.4 = (bf16[512,256]{1,0:T(8,128)(2,1)S(1)}, bf16[512,256]{1,0:T(8,128)(2,1)S(1)}, u32[]{:S(2)}, u32[]{:S(2)}) collective-permute-start(bf16[512,256]{1,0:T(8,128)(2,1)S(1)} %fusion.4), channel_id=1, source_target_pairs={{0,8},{1,9},{2,10},{3,11},{4,12},{5,13},{6,14},{7,15},{8,16},{9,17... | collective-permute-start | bytes 786440 | tf_op jit(solution)/shard_map/ppermute | solution.py:345
  75.7 20.4 %collective-permute-start.5 = (bf16[512,256]{1,0:T(8,128)(2,1)S(1)}, bf16[512,256]{1,0:T(8,128)(2,1)S(1)}, u32[]{:S(2)}, u32[]{:S(2)}) collective-permute-start(bf16[512,256]{1,0:T(8,128)(2,1)S(1)} %fusion.4), channel_id=1, source_target_pairs={{0,16},{1,17},{2,18},{3,19},{4,20},{5,21},{6,22},{7,23},{8,24},{9,... | collective-permute-start | bytes 786440 | tf_op jit(solution)/shard_map/ppermute | solution.py:345
  78.8 17.3 %collective-permute-start.6 = (bf16[512,256]{1,0:T(8,128)(2,1)S(1)}, bf16[512,256]{1,0:T(8,128)(2,1)S(1)}, u32[]{:S(2)}, u32[]{:S(2)}) collective-permute-start(bf16[512,256]{1,0:T(8,128)(2,1)S(1)} %fusion.4), channel_id=1, source_target_pairs={{0,24},{1,25},{2,26},{3,27},{4,28},{5,29},{6,30},{7,31},{8,0},{9,1... | collective-permute-start | bytes 786440 | tf_op jit(solution)/shard_map/ppermute | solution.py:345
  86.8 9.2 %collective-permute-start.17 = (bf16[256,256]{1,0:T(8,128)(2,1)S(1)}, bf16[256,256]{1,0:T(8,128)(2,1)S(1)}, u32[]{:S(2)}, u32[]{:S(2)}) collective-permute-start(bf16[256,256]{1,0:T(8,128)(2,1)S(1)} %get-tuple-element.71), channel_id=1, source_target_pairs={{0,4},{1,5},{2,6},{3,7},{4,0},{5,1},{6,2},{7,3},{8,12},{9,13},{10,... | collective-permute-start | bytes 393224 | tf_op jit(solution)/shard_map/ppermute | solution.py:345
  97.9 7.6 %collective-permute-start.18 = (bf16[4,512,256]{2,1,0:T(8,128)(2,1)}, bf16[4,512,256]{2,1,0:T(8,128)(2,1)}, u32[]{:S(2)}, u32[]{:S(2)}) collective-permute-start(bf16[4,512,256]{2,1,0:T(8,128)(2,1)} %pad_maximum_fusion.refs_0_), channel_id=1, source_target_pairs={{0,1},{1,0},{2,3},{3,2},{4,5},{5,4},{6,7},{7,6},{8,9},{9,8},{10,11... | collective-permute-start | bytes 3145736 | tf_op jit(solution)/shard_map/ppermute | solution.py:345
  97.9 44.2 %collective-permute-start.19 = (bf16[4,512,256]{2,1,0:T(8,128)(2,1)}, bf16[4,512,256]{2,1,0:T(8,128)(2,1)}, u32[]{:S(2)}, u32[]{:S(2)}) collective-permute-start(bf16[4,512,256]{2,1,0:T(8,128)(2,1)} %pad_maximum_fusion.refs_0_), channel_id=1, source_target_pairs={{0,4},{1,5},{2,6},{3,7},{4,0},{5,1},{6,2},{7,3},{8,12},{9,13},{10,... | collective-permute-start | bytes 3145736 | tf_op jit(solution)/shard_map/ppermute | solution.py:345
  99.3 10.4 %collective-permute-start.22 = (bf16[256,256]{1,0:T(8,128)(2,1)S(1)}, bf16[256,256]{1,0:T(8,128)(2,1)S(1)}, u32[]{:S(2)}, u32[]{:S(2)}) collective-permute-start(bf16[256,256]{1,0:T(8,128)(2,1)S(1)} %add_convert_fusion.3.refs_9_), channel_id=1, source_target_pairs={{0,8},{1,9},{2,10},{3,11},{4,12},{5,13},{6,14},{7,15},{8,16},{9,17... | collective-permute-start | bytes 393224 | tf_op jit(solution)/shard_map/ppermute | solution.py:345
  107.6 34.5 %collective-permute-start.20 = (bf16[2,512,256]{2,1,0:T(8,128)(2,1)}, bf16[2,512,256]{2,1,0:T(8,128)(2,1)}, u32[]{:S(2)}, u32[]{:S(2)}) collective-permute-start(bf16[2,512,256]{2,1,0:T(8,128)(2,1)} %dynamic-slice_select_fusion), channel_id=1, source_target_pairs={{0,2},{1,3},{2,0},{3,1},{4,6},{5,7},{6,4},{7,5},{8,10},{9,11},{10,... | collective-permute-start | bytes 1572872 | tf_op jit(solution)/shard_map/ppermute | solution.py:345
  109.1 33.0 %collective-permute-start.21 = (bf16[2,512,256]{2,1,0:T(8,128)(2,1)}, bf16[2,512,256]{2,1,0:T(8,128)(2,1)}, u32[]{:S(2)}, u32[]{:S(2)}) collective-permute-start(bf16[2,512,256]{2,1,0:T(8,128)(2,1)} %dynamic-slice_select_fusion), channel_id=1, source_target_pairs={{0,3},{1,2},{2,1},{3,0},{4,7},{5,6},{6,5},{7,4},{8,11},{9,10},{10,... | collective-permute-start | bytes 1572872 | tf_op jit(solution)/shard_map/ppermute | solution.py:345
  109.3 32.8 %collective-permute-start.23 = (bf16[256,256]{1,0:T(8,128)(2,1)S(1)}, bf16[256,256]{1,0:T(8,128)(2,1)S(1)}, u32[]{:S(2)}, u32[]{:S(2)}) collective-permute-start(bf16[256,256]{1,0:T(8,128)(2,1)S(1)} %add_convert_fusion.3.refs_9_), channel_id=1, source_target_pairs={{0,16},{1,17},{2,18},{3,19},{4,20},{5,21},{6,22},{7,23},{8,24},{9,... | collective-permute-start | bytes 393224 | tf_op jit(solution)/shard_map/ppermute | solution.py:345
  109.7 32.3 %collective-permute-start.24 = (bf16[256,256]{1,0:T(8,128)(2,1)S(1)}, bf16[256,256]{1,0:T(8,128)(2,1)S(1)}, u32[]{:S(2)}, u32[]{:S(2)}) collective-permute-start(bf16[256,256]{1,0:T(8,128)(2,1)S(1)} %add_convert_fusion.3.refs_9_), channel_id=1, source_target_pairs={{0,24},{1,25},{2,26},{3,27},{4,28},{5,29},{6,30},{7,31},{8,0},{9,1... | collective-permute-start | bytes 393224 | tf_op jit(solution)/shard_map/ppermute | solution.py:345
  113.1 29.0 %copy-start.3 = (f32[2048,256]{1,0:T(8,128)S(1)}, f32[2048,256]{1,0:T(8,128)}, u32[]{:S(2)}) copy-start(f32[2048,256]{1,0:T(8,128)} %refs_7_.1) | copy-start | bytes 6291460
  150.4 1.2 collective-permute-start.25
  151.6 3.6 %collective-permute-start.26 = (f32[4,256]{1,0:T(4,128)S(1)}, f32[4,256]{1,0:T(4,128)S(1)}, u32[]{:S(2)}, u32[]{:S(2)}) collective-permute-start(f32[4,256]{1,0:T(4,128)S(1)} %add.207), channel_id=1, source_target_pairs={{0,2},{1,3},{2,0},{3,1},{4,6},{5,7},{6,4},{7,5},{8,10},{9,11},{10,... | collective-permute-start | bytes 12296 | tf_op jit(solution)/shard_map/ppermute | solution.py:345
  155.2 3.6 %collective-permute-start.27 = (f32[4,256]{1,0:T(4,128)S(1)}, f32[4,256]{1,0:T(4,128)S(1)}, u32[]{:S(2)}, u32[]{:S(2)}) collective-permute-start(f32[4,256]{1,0:T(4,128)S(1)} %add.208), channel_id=1, source_target_pairs={{0,4},{1,5},{2,6},{3,7},{4,0},{5,1},{6,2},{7,3},{8,12},{9,13},{10,... | collective-permute-start | bytes 12296 | tf_op jit(solution)/shard_map/ppermute | solution.py:345
  158.8 5.4 %collective-permute-start.28 = (f32[4,256]{1,0:T(4,128)S(1)}, f32[4,256]{1,0:T(4,128)S(1)}, u32[]{:S(2)}, u32[]{:S(2)}) collective-permute-start(f32[4,256]{1,0:T(4,128)S(1)} %add.209), channel_id=1, source_target_pairs={{0,8},{1,9},{2,10},{3,11},{4,12},{5,13},{6,14},{7,15},{8,16},{9,17... | collective-permute-start | bytes 12296 | tf_op jit(solution)/shard_map/ppermute | solution.py:345
  158.8 5.4 %collective-permute-start.29 = (f32[4,256]{1,0:T(4,128)S(1)}, f32[4,256]{1,0:T(4,128)S(1)}, u32[]{:S(2)}, u32[]{:S(2)}) collective-permute-start(f32[4,256]{1,0:T(4,128)S(1)} %add.209), channel_id=1, source_target_pairs={{0,16},{1,17},{2,18},{3,19},{4,20},{5,21},{6,22},{7,23},{8,24},{9,... | collective-permute-start | bytes 12296 | tf_op jit(solution)/shard_map/ppermute | solution.py:345
  159.1 5.7 %collective-permute-start.30 = (f32[4,256]{1,0:T(4,128)S(1)}, f32[4,256]{1,0:T(4,128)S(1)}, u32[]{:S(2)}, u32[]{:S(2)}) collective-permute-start(f32[4,256]{1,0:T(4,128)S(1)} %add.209), channel_id=1, source_target_pairs={{0,24},{1,25},{2,26},{3,27},{4,28},{5,29},{6,30},{7,31},{8,0},{9,1... | collective-permute-start | bytes 12296 | tf_op jit(solution)/shard_map/ppermute | solution.py:345
  (10 other events, 69.9 us)
where the time goes:
time: 169 us
  Pallas kernels  59.6 us (35%)
  starting transfers between devices  46.7 us (28%)
  waiting for transfers between devices  41.4 us (24%)
  other arithmetic  12.6 us (7%)
  local copies, waits for them, and re-layouts  4.25 us (3%)
  matrix products  3.38 us (2%)
    ppermute x31, starting transfers between devices, move(): return lax.ppermute(value, ('row', 'col'), pairs)  46.7 us
    ppermute x31, waiting for transfers between devices, move(): return lax.ppermute(value, ('row', 'col'), pairs)  41.4 us
    pallas_call x1, Pallas kernels, update_gram(): pl.pallas_call(functools.partial(gram_kernel, scale, block, first), grid_...  28.9 us
    pallas_call x2, Pallas kernels, back_product(): pl.pallas_call(functools.partial(back_kernel, streams), grid_spec=pltpu.P...  17.3 us
    pallas_call x1, Pallas kernels, tail(): pl.pallas_call(functools.partial(tail_kernel, scale, even, len(copies)),...  7.02 us
    pallas_call x1, Pallas kernels, build_grads(): pl.pallas_call(functools.partial(grads_kernel, parts, cols // rank, rows...  6.39 us
    sub x1, other arithmetic, shards(): (step + step_next * (1.0 + momentum)) * queries - step_next * step * mapped  3.97 us
    unnamed x23, local copies, waits for them, and re-layouts  3.93 us
  transfers between devices with their start and end apart: 31, of which 11 were waited for; matrix products, arithmetic and copies ran while one was open for 7% of the time, Pallas kernels for 26%

commit v1 on v0

--- a/solution.py
+++ b/solution.py
@@ -157,23 +157,30 @@
 def gram_kernel(scale, block, first, at_ref, gram_ref, left_ref, right_ref, *rest):
     out_ref, copy_ref = rest[-2:]
     strip = copy_ref.shape[1] // 3
+    cols = gram_ref.shape[1]
     lower = ((first + pl.program_id(0)) * block >= strip).astype(jnp.int32)
     left = left_ref[...]
-    offset = at_ref[0] + (first + pl.program_id(0)) * block
-    ahead = lax.broadcasted_iota(jnp.int32, (block, strip), 0)
-    ahead = ahead - lax.broadcasted_iota(jnp.int32, (block, strip), 1)
-    for s in range(gram_ref.shape[1] // strip):
+    for s in range(cols // strip):
         part = slice(s * strip, (s + 1) * strip)
         product = dot(left, right_ref[:, part], ((0,), (0,)))
-        value = decay_rate * gram_ref[:, part] + scale * product
-        value = value + jnp.where(ahead == s * strip - offset, damping, 0.0)
-        out_ref[:, part] = value
-        short = value.astype(BF)
-        for k in range(3):
-
-            @pl.when(at_ref[1 + 3 * lower + k] == s)
-            def _(k=k, short=short):
-                copy_ref[:, k * strip : (k + 1) * strip] = short
+        out_ref[:, part] = decay_rate * gram_ref[:, part] + scale * product
+
+    start = at_ref[0] + (first + pl.program_id(0)) * block
+
+    @pl.when((start >= 0) & (start < cols))
+    def _():
+        here = lax.broadcasted_iota(jnp.int32, (block, block), 0)
+        here = here == lax.broadcasted_iota(jnp.int32, (block, block), 1)
+        place = pl.ds(pl.multiple_of(start, block), block)
+        out_ref[:, place] = out_ref[:, place] + jnp.where(here, damping, 0.0)
+
+    for k in range(3):
+        wanted = at_ref[1 + 3 * lower + k]
+
+        @pl.when(wanted >= 0)
+        def _(k=k, wanted=wanted):
+            place = pl.ds(pl.multiple_of(wanted * strip, strip), strip)
+            copy_ref[:, k * strip : (k + 1) * strip] = out_ref[:, place].astype(BF)
 
 
 def update_gram(at, gram, left, right, scale, first, count, block, before):

time: 169 us -> 166 us (0.982)
  Pallas kernels: 59.6 us -> 56 us
    pallas_call x1, Pallas kernels: 28.9 us -> 25.3 us  [update_gram(): pl.pallas_call(functools.partial(gram_kernel, scale, block, first), grid_...]
  transfers between devices with their start and end apart: 31 -> 31, of which waited for: 11 -> 11; matrix products, arithmetic and copies ran while one was open for 7% -> 7% of each run, Pallas kernels for 26% -> 24%
where the time goes in v1:
time: 166 us; the launch traced here: 165 us
  Pallas kernels  56 us (34%)
  starting transfers between devices  46.6 us (28%)
  waiting for transfers between devices  41.5 us (25%)
  other arithmetic  12.6 us (8%)
  local copies, waits for them, and re-layouts  4.25 us (3%)
  matrix products  3.38 us (2%)
    ppermute x31, starting transfers between devices, move(): return lax.ppermute(value, ('row', 'col'), pairs)  46.6 us
    ppermute x31, waiting for transfers between devices, move(): return lax.ppermute(value, ('row', 'col'), pairs)  41.5 us
    pallas_call x1, Pallas kernels, update_gram(): pl.pallas_call(functools.partial(gram_kernel, scale, block, first), grid_...  25.3 us
    pallas_call x2, Pallas kernels, back_product(): pl.pallas_call(functools.partial(back_kernel, streams), grid_spec=pltpu.P...  17.3 us
    pallas_call x1, Pallas kernels, tail(): pl.pallas_call(functools.partial(tail_kernel, scale, even, len(copies)),...  7.02 us
    pallas_call x1, Pallas kernels, build_grads(): pl.pallas_call(functools.partial(grads_kernel, parts, cols // rank, rows...  6.39 us
    sub x1, other arithmetic, shards(): (step + step_next * (1.0 + momentum)) * queries - step_next * step * mapped  3.97 us
    unnamed x23, local copies, waits for them, and re-layouts  3.93 us
  transfers between devices with their start and end apart: 31, of which 11 were waited for; matrix products, arithmetic and copies ran while one was open for 7% of the time, Pallas kernels for 24%

profile of v1, /device:TPU:0, one launch (start us, length us, event | category | flops | bytes accessed | tf_op | source)
XLA Modules:
  0.0 165.2 jit_solution(11029182424090811557)
XLA Ops:
  0.7 1.9 %copy.10 = bf16[2048,256]{0,1:T(8,128)(2,1)S(1)} copy(f32[2048,256]{1,0:T(8,128)} %refs_7_.1) | data formatting | bytes 3145728 | tf_op args[6]
  2.7 9.1 %back_product.2 = bf16[2048,256]{1,0:T(8,128)(2,1)} custom-call(s32[2]{0:T(128)S(1)} %get-tuple-element.74.plan_ref, bf16[256,2048]{1,0:T(8,128)(2,1)S(1)} %bitcast.105, f32[2048,4096]{1,0:T(8,128)} %gram_ref.1, f32[2048,4096]{1,0:T(8,128)} %gram_ref.1), custom_call_target="tpu_custom_call" | custom-call | flops 2147483648 | bytes 18874368 | tf_op jit(solution)/shard_map/back_product/pallas_call | solution.py:142
  11.7 3.0 %collective-permute-start = (bf16[2048,256]{1,0:T(8,128)(2,1)}, bf16[2048,256]{1,0:T(8,128)(2,1)}, u32[]{:S(2)}, u32[]{:S(2)}) collective-permute-start(bf16[2048,256]{1,0:T(8,128)(2,1)} %back_product.2), channel_id=1, source_target_pairs={{0,4},{1,5},{2,6},{3,7},{4,0},{5,1},{6,2},{7,3},{8,12},{9,13},{10,... | collective-permute-start | bytes 3145736 | tf_op jit(solution)/shard_map/ppermute | solution.py:352
  14.9 2.2 %fusion.1 = bf16[16,2,8,128]{3,2,1,0:T(8,128)(2,1)S(1)} fusion(bf16[4096,128]{1,0:T(8,128)(2,1)} %param.10, bf16[256,4096]{1,0:T(8,128)(2,1)S(1)} %copy-done, pred[256]{0:T(512)(128)(4,1)S(1)} %fusion.10), kind=kOutput, calls=%fused_computation.4 | convolution fusion | flops 268500992 | bytes 3211520 | tf_op jit(solution)/shard_map/dot_general | solution.py:21
  17.9 1.6 collective-permute-start.7
  19.5 2.6 %collective-permute-start.8 = (bf16[512,128]{1,0:T(8,128)(2,1)S(1)}, bf16[512,128]{1,0:T(8,128)(2,1)S(1)}, u32[]{:S(2)}, u32[]{:S(2)}) collective-permute-start(bf16[512,128]{1,0:T(8,128)(2,1)S(1)} %pad_maximum_fusion.2), channel_id=1, source_target_pairs={{0,16},{1,17},{2,18},{3,19},{4,20},{5,21},{6,22},{7,23},{8,24},{9,... | collective-permute-start | bytes 393224 | tf_op jit(solution)/shard_map/ppermute | solution.py:352
  22.1 1.3 collective-permute-start.9
  23.4 8.2 %back_product.3 = f32[2048,256]{1,0:T(8,128)S(1)} custom-call(s32[2]{0:T(128)S(1)} %get-tuple-element.34.plan_ref, bf16[256,2048]{1,0:T(8,128)(2,1)S(1)} %bitcast.106, f32[2048,4096]{1,0:T(8,128)} %gram_ref.1, f32[2048,4096]{1,0:T(8,128)} %gram_ref.1, f32[2048,256]{1,0:T(8,128)S(1)} %copy-done.2), custom_call_target="tpu_custom_call" | custom-call | flops 2147483648 | bytes 18874368 | tf_op jit(solution)/shard_map/back_product/pallas_call | solution.py:142
  32.6 1.5 collective-permute-start.11
  34.0 4.1 %collective-permute-done = bf16[2048,256]{1,0:T(8,128)(2,1)} collective-permute-done((bf16[2048,256]{1,0:T(8,128)(2,1)}, bf16[2048,256]{1,0:T(8,128)(2,1)}, u32[]{:S(2)}, u32[]{:S(2)}) %collective-permute-start) | collective-permute-done | bytes 1048608 | tf_op jit(solution)/shard_map/ppermute | solution.py:352
  38.2 2.1 %fusion.7 = (bf16[512,256]{1,0:T(8,128)(2,1)}, bf16[512,256]{1,0:T(8,128)(2,1)S(1)}, bf16[512,256]{1,0:T(8,128)(2,1)}) fusion(f32[4,512,256]{2,1,0:T(8,128)S(1)} %bitcast.107, s32[]{:T(128)S(6)} %select_n.130, bf16[4,512,256]{2,1,0:T(8,128)(2,1)} %bitcast.13, s32[]{:T(128)S(6)} %select_n.134, s32[]{:T(128)S(6)} %select_n.132), kind=kLoop, calls=%fused_computation.18 | loop fusion | flops 1179648 | bytes 3145740 | tf_op jit(solution)/shard_map/convert_element_type | solution.py:395
  40.3 5.2 %collective-permute-done.11.refs_2_ = bf16[4,512,128]{2,1,0:T(8,128)(2,1)} collective-permute-done((bf16[4,512,128]{2,1,0:T(8,128)(2,1)}, bf16[4,512,128]{2,1,0:T(8,128)(2,1)}, u32[]{:S(2)}, u32[]{:S(2)}) %collective-permute-start.11) | collective-permute-done | bytes 524320 | tf_op jit(solution)/shard_map/ppermute | solution.py:352
  45.9 1.5 collective-permute-start.10
  47.5 3.5 %collective-permute-start.1 = (bf16[512,256]{1,0:T(8,128)(2,1)}, bf16[512,256]{1,0:T(8,128)(2,1)}, u32[]{:S(2)}, u32[]{:S(2)}) collective-permute-start(bf16[512,256]{1,0:T(8,128)(2,1)} %get-tuple-element.68), channel_id=1, source_target_pairs={{0,8},{1,9},{2,10},{3,11},{4,12},{5,13},{6,14},{7,15},{8,16},{9,17... | collective-permute-start | bytes 786440 | tf_op jit(solution)/shard_map/ppermute | solution.py:352
  50.9 2.4 %collective-permute-start.3 = (bf16[512,256]{1,0:T(8,128)(2,1)S(1)}, bf16[512,256]{1,0:T(8,128)(2,1)}, u32[]{:S(2)}, u32[]{:S(2)}) collective-permute-start(bf16[512,256]{1,0:T(8,128)(2,1)S(1)} %get-tuple-element.69), channel_id=1, source_target_pairs={{0,24},{1,25},{2,26},{3,27},{4,28},{5,29},{6,30},{7,31},{8,0},{9,1... | collective-permute-start | bytes 786440 | tf_op jit(solution)/shard_map/ppermute | solution.py:352
  53.3 5.5 %collective-permute-done.1 = bf16[512,256]{1,0:T(8,128)(2,1)} collective-permute-done((bf16[512,256]{1,0:T(8,128)(2,1)}, bf16[512,256]{1,0:T(8,128)(2,1)}, u32[]{:S(2)}, u32[]{:S(2)}) %collective-permute-start.1) | collective-permute-done | bytes 262176 | tf_op jit(solution)/shard_map/ppermute | solution.py:352
  58.8 8.2 %collective-permute-done.2 = bf16[512,256]{1,0:T(8,128)(2,1)} collective-permute-done((bf16[512,256]{1,0:T(8,128)(2,1)}, bf16[512,256]{1,0:T(8,128)(2,1)}, u32[]{:S(2)}, u32[]{:S(2)}) %collective-permute-start.2) | collective-permute-done | bytes 262176 | tf_op jit(solution)/shard_map/ppermute | solution.py:352
  69.7 5.9 %collective-permute-start.4 = (bf16[512,256]{1,0:T(8,128)(2,1)S(1)}, bf16[512,256]{1,0:T(8,128)(2,1)S(1)}, u32[]{:S(2)}, u32[]{:S(2)}) collective-permute-start(bf16[512,256]{1,0:T(8,128)(2,1)S(1)} %fusion.4), channel_id=1, source_target_pairs={{0,8},{1,9},{2,10},{3,11},{4,12},{5,13},{6,14},{7,15},{8,16},{9,17... | collective-permute-start | bytes 786440 | tf_op jit(solution)/shard_map/ppermute | solution.py:352
  75.7 3.1 %collective-permute-start.5 = (bf16[512,256]{1,0:T(8,128)(2,1)S(1)}, bf16[512,256]{1,0:T(8,128)(2,1)S(1)}, u32[]{:S(2)}, u32[]{:S(2)}) collective-permute-start(bf16[512,256]{1,0:T(8,128)(2,1)S(1)} %fusion.4), channel_id=1, source_target_pairs={{0,16},{1,17},{2,18},{3,19},{4,20},{5,21},{6,22},{7,23},{8,24},{9,... | collective-permute-start | bytes 786440 | tf_op jit(solution)/shard_map/ppermute | solution.py:352
  80.0 6.4 %build_grads.1 = (bf16[256,4096]{1,0:T(8,128)(2,1)S(1)}, bf16[256,2048]{1,0:T(8,128)(2,1)S(1)}) custom-call(s32[2]{0:T(128)S(1)} %pad_add_fusion.2.at_ref, bf16[4,512,128]{2,1,0:T(8,128)(2,1)} %pad_maximum_fusion.1.refs_0_, bf16[4,512,128]{2,1,0:T(8,128)(2,1)} %collective-permute-done.10.refs_1_, bf16[4,512,128]{2,1,0:T(8,128)(2,1)} %collective-permute-done.11.refs_2_, ...), custom_call_target="tpu_custom_call" | custom-call | flops 805306368 | bytes 3145728 | tf_op jit(solution)/shard_map/build_grads/pallas_call | solution.py:88
  87.4 8.7 %collective-permute-done.5 = bf16[512,256]{1,0:T(8,128)(2,1)S(1)} collective-permute-done((bf16[512,256]{1,0:T(8,128)(2,1)S(1)}, bf16[512,256]{1,0:T(8,128)(2,1)S(1)}, u32[]{:S(2)}, u32[]{:S(2)}) %collective-permute-start.5) | collective-permute-done | bytes 262176 | tf_op jit(solution)/shard_map/ppermute | solution.py:352
  99.3 6.1 %collective-permute-start.22 = (bf16[256,256]{1,0:T(8,128)(2,1)S(1)}, bf16[256,256]{1,0:T(8,128)(2,1)S(1)}, u32[]{:S(2)}, u32[]{:S(2)}) collective-permute-start(bf16[256,256]{1,0:T(8,128)(2,1)S(1)} %add_convert_fusion.3.refs_9_), channel_id=1, source_target_pairs={{0,8},{1,9},{2,10},{3,11},{4,12},{5,13},{6,14},{7,15},{8,16},{9,17... | collective-permute-start | bytes 393224 | tf_op jit(solution)/shard_map/ppermute | solution.py:352
  105.5 2.1 %dynamic-slice_select_fusion = bf16[2,512,256]{2,1,0:T(8,128)(2,1)} fusion(bf16[4,512,256]{2,1,0:T(8,128)(2,1)} %collective-permute-done.18.refs_2_, s32[]{:T(128)S(6)} %select_n.136, bf16[4,512,256]{2,1,0:T(8,128)(2,1)} %pad_maximum_fusion.refs_0_, pred[]{:T(512)S(6)} %eq.29), kind=kLoop, calls=%fused_computation.6 | loop fusion | flops 262144 | bytes 1572869 | tf_op jit(solution)/shard_map/jit(_where)/select_n | solution.py:428
  107.6 1.5 collective-permute-start.20
  109.7 3.4 %collective-permute-start.24 = (bf16[256,256]{1,0:T(8,128)(2,1)S(1)}, bf16[256,256]{1,0:T(8,128)(2,1)S(1)}, u32[]{:S(2)}, u32[]{:S(2)}) collective-permute-start(bf16[256,256]{1,0:T(8,128)(2,1)S(1)} %add_convert_fusion.3.refs_9_), channel_id=1, source_target_pairs={{0,24},{1,25},{2,26},{3,27},{4,28},{5,29},{6,30},{7,31},{8,0},{9,1... | collective-permute-start | bytes 393224 | tf_op jit(solution)/shard_map/ppermute | solution.py:352
  113.1 25.3 %update_gram.1 = (f32[2048,4096]{1,0:T(8,128)}, bf16[2048,3072]{1,0:T(8,128)(2,1)S(1)}) custom-call(s32[7]{0:T(128)S(1)} %stack.128.at_ref, f32[2048,4096]{1,0:T(8,128)} %gram_ref.1, bf16[256,2048]{1,0:T(8,128)(2,1)S(1)} %copy-done.5, bf16[256,4096]{1,0:T(8,128)(2,1)S(1)} %get-tuple-element.51.right_ref.refs_5_), custom_call_target="tpu_custom_call" | custom-call | flops 4294967296 | bytes 67108864 | tf_op jit(solution)/shard_map/update_gram/pallas_call | solution.py:201
  138.5 7.0 %tail.1 = (f32[2048,256]{1,0:T(8,128)S(1)}, f32[4,256]{1,0:T(4,128)S(1)}) custom-call(s32[9]{0:T(128)S(1)} %concatenate.7.plan_ref, bf16[4,512,256]{2,1,0:T(8,128)(2,1)} %pad_maximum_fusion.refs_0_, bf16[4,512,256]{2,1,0:T(8,128)(2,1)} %collective-permute-done.19.refs_1_, bf16[4,512,256]{2,1,0:T(8,128)(2,1)} %collective-permute-done.18.refs_2_, ...), custom_call_target="tpu_custom_call" | custom-call | flops 4294967296 | bytes 16777216 | tf_op jit(solution)/shard_map/tail/pallas_call | solution.py:299
  148.6 3.0 %collective-permute-done.26 = f32[4,256]{1,0:T(4,128)S(1)} collective-permute-done((f32[4,256]{1,0:T(4,128)S(1)}, f32[4,256]{1,0:T(4,128)S(1)}, u32[]{:S(2)}, u32[]{:S(2)}) %collective-permute-start.26) | collective-permute-done | bytes 4128 | tf_op jit(solution)/shard_map/ppermute | solution.py:352
  152.1 3.1 %collective-permute-done.27 = f32[4,256]{1,0:T(4,128)S(1)} collective-permute-done((f32[4,256]{1,0:T(4,128)S(1)}, f32[4,256]{1,0:T(4,128)S(1)}, u32[]{:S(2)}, u32[]{:S(2)}) %collective-permute-start.27) | collective-permute-done | bytes 4128 | tf_op jit(solution)/shard_map/ppermute | solution.py:352
  155.5 3.5 %collective-permute-start.30 = (f32[4,256]{1,0:T(4,128)S(1)}, f32[4,256]{1,0:T(4,128)S(1)}, u32[]{:S(2)}, u32[]{:S(2)}) collective-permute-start(f32[4,256]{1,0:T(4,128)S(1)} %add.209), channel_id=1, source_target_pairs={{0,24},{1,25},{2,26},{3,27},{4,28},{5,29},{6,30},{7,31},{8,0},{9,1... | collective-permute-start | bytes 12296 | tf_op jit(solution)/shard_map/ppermute | solution.py:352
  159.0 1.6 collective-permute-done.28
  161.3 4.0 %multiply_subtract_fusion = f32[2048,256]{1,0:T(8,128)} fusion(f32[2048,256]{1,0:T(8,128)} %copy-done.6, f32[2048,256]{1,0:T(8,128)} %refs_7_.1, f32[256]{0:T(256)S(1)} %bitcast.119, f32[256]{0:T(256)S(1)} %bitcast.120), kind=kLoop, calls=%fused_computation | loop fusion | flops 1572864 | bytes 6293504 | tf_op jit(solution)/shard_map/sub | solution.py:481
  (85 shorter events, 15.6 us)
Async XLA Ops:
  11.7 26.4 %collective-permute-start = (bf16[2048,256]{1,0:T(8,128)(2,1)}, bf16[2048,256]{1,0:T(8,128)(2,1)}, u32[]{:S(2)}, u32[]{:S(2)}) collective-permute-start(bf16[2048,256]{1,0:T(8,128)(2,1)} %back_product.2), channel_id=1, source_target_pairs={{0,4},{1,5},{2,6},{3,7},{4,0},{5,1},{6,2},{7,3},{8,12},{9,13},{10,... | collective-permute-start | bytes 3145736 | tf_op jit(solution)/shard_map/ppermute | solution.py:352
  17.9 13.8 %collective-permute-start.7 = (bf16[512,128]{1,0:T(8,128)(2,1)S(1)}, bf16[512,128]{1,0:T(8,128)(2,1)S(1)}, u32[]{:S(2)}, u32[]{:S(2)}) collective-permute-start(bf16[512,128]{1,0:T(8,128)(2,1)S(1)} %pad_maximum_fusion.2), channel_id=1, source_target_pairs={{0,8},{1,9},{2,10},{3,11},{4,12},{5,13},{6,14},{7,15},{8,16},{9,17... | collective-permute-start | bytes 393224 | tf_op jit(solution)/shard_map/ppermute | solution.py:352
  19.5 12.2 %collective-permute-start.8 = (bf16[512,128]{1,0:T(8,128)(2,1)S(1)}, bf16[512,128]{1,0:T(8,128)(2,1)S(1)}, u32[]{:S(2)}, u32[]{:S(2)}) collective-permute-start(bf16[512,128]{1,0:T(8,128)(2,1)S(1)} %pad_maximum_fusion.2), channel_id=1, source_target_pairs={{0,16},{1,17},{2,18},{3,19},{4,20},{5,21},{6,22},{7,23},{8,24},{9,... | collective-permute-start | bytes 393224 | tf_op jit(solution)/shard_map/ppermute | solution.py:352
  22.1 9.6 %collective-permute-start.9 = (bf16[512,128]{1,0:T(8,128)(2,1)S(1)}, bf16[512,128]{1,0:T(8,128)(2,1)S(1)}, u32[]{:S(2)}, u32[]{:S(2)}) collective-permute-start(bf16[512,128]{1,0:T(8,128)(2,1)S(1)} %pad_maximum_fusion.2), channel_id=1, source_target_pairs={{0,24},{1,25},{2,26},{3,27},{4,28},{5,29},{6,30},{7,31},{8,0},{9,1... | collective-permute-start | bytes 393224 | tf_op jit(solution)/shard_map/ppermute | solution.py:352
  32.6 12.9 %collective-permute-start.11 = (bf16[4,512,128]{2,1,0:T(8,128)(2,1)}, bf16[4,512,128]{2,1,0:T(8,128)(2,1)}, u32[]{:S(2)}, u32[]{:S(2)}) collective-permute-start(bf16[4,512,128]{2,1,0:T(8,128)(2,1)} %pad_maximum_fusion.1.refs_0_), channel_id=1, source_target_pairs={{0,2},{1,3},{2,0},{3,1},{4,6},{5,7},{6,4},{7,5},{8,10},{9,11},{10,... | collective-permute-start | bytes 1572872 | tf_op jit(solution)/shard_map/ppermute | solution.py:352
  45.4 23.0 %collective-permute-start.12 = (bf16[4,512,128]{2,1,0:T(8,128)(2,1)}, bf16[4,512,128]{2,1,0:T(8,128)(2,1)}, u32[]{:S(2)}, u32[]{:S(2)}) collective-permute-start(bf16[4,512,128]{2,1,0:T(8,128)(2,1)} %collective-permute-done.11.refs_2_), channel_id=1, source_target_pairs={{0,4},{1,5},{2,6},{3,7},{4,0},{5,1},{6,2},{7,3},{8,12},{9,13},{10,... | collective-permute-start | bytes 1572872 | tf_op jit(solution)/shard_map/ppermute | solution.py:352
  45.9 22.7 %collective-permute-start.10 = (bf16[4,512,128]{2,1,0:T(8,128)(2,1)}, bf16[4,512,128]{2,1,0:T(8,128)(2,1)}, u32[]{:S(2)}, u32[]{:S(2)}) collective-permute-start(bf16[4,512,128]{2,1,0:T(8,128)(2,1)} %pad_maximum_fusion.1.refs_0_), channel_id=1, source_target_pairs={{0,4},{1,5},{2,6},{3,7},{4,0},{5,1},{6,2},{7,3},{8,12},{9,13},{10,... | collective-permute-start | bytes 1572872 | tf_op jit(solution)/shard_map/ppermute | solution.py:352
  47.5 11.4 %collective-permute-start.1 = (bf16[512,256]{1,0:T(8,128)(2,1)}, bf16[512,256]{1,0:T(8,128)(2,1)}, u32[]{:S(2)}, u32[]{:S(2)}) collective-permute-start(bf16[512,256]{1,0:T(8,128)(2,1)} %get-tuple-element.68), channel_id=1, source_target_pairs={{0,8},{1,9},{2,10},{3,11},{4,12},{5,13},{6,14},{7,15},{8,16},{9,17... | collective-permute-start | bytes 786440 | tf_op jit(solution)/shard_map/ppermute | solution.py:352
  50.9 16.1 %collective-permute-start.2 = (bf16[512,256]{1,0:T(8,128)(2,1)}, bf16[512,256]{1,0:T(8,128)(2,1)}, u32[]{:S(2)}, u32[]{:S(2)}) collective-permute-start(bf16[512,256]{1,0:T(8,128)(2,1)} %get-tuple-element.70), channel_id=1, source_target_pairs={{0,16},{1,17},{2,18},{3,19},{4,20},{5,21},{6,22},{7,23},{8,24},{9,... | collective-permute-start | bytes 786440 | tf_op jit(solution)/shard_map/ppermute | solution.py:352
  50.9 16.1 %collective-permute-start.3 = (bf16[512,256]{1,0:T(8,128)(2,1)S(1)}, bf16[512,256]{1,0:T(8,128)(2,1)}, u32[]{:S(2)}, u32[]{:S(2)}) collective-permute-start(bf16[512,256]{1,0:T(8,128)(2,1)S(1)} %get-tuple-element.69), channel_id=1, source_target_pairs={{0,24},{1,25},{2,26},{3,27},{4,28},{5,29},{6,30},{7,31},{8,0},{9,1... | collective-permute-start | bytes 786440 | tf_op jit(solution)/shard_map/ppermute | solution.py:352
  68.6 7.0 %collective-permute-start.13 = (bf16[4,512,128]{2,1,0:T(8,128)(2,1)}, bf16[4,512,128]{2,1,0:T(8,128)(2,1)S(1)}, u32[]{:S(2)}, u32[]{:S(2)}) collective-permute-start(bf16[4,512,128]{2,1,0:T(8,128)(2,1)} %pad_maximum_fusion.1.refs_0_), channel_id=1, source_target_pairs={{0,1},{1,0},{2,3},{3,2},{4,5},{5,4},{6,7},{7,6},{8,9},{9,8},{10,11... | collective-permute-start | bytes 1572872 | tf_op jit(solution)/shard_map/ppermute | solution.py:352
  68.6 10.1 %collective-permute-start.14 = (bf16[4,512,128]{2,1,0:T(8,128)(2,1)}, bf16[4,512,128]{2,1,0:T(8,128)(2,1)S(1)}, u32[]{:S(2)}, u32[]{:S(2)}) collective-permute-start(bf16[4,512,128]{2,1,0:T(8,128)(2,1)} %collective-permute-done.10.refs_1_), channel_id=1, source_target_pairs={{0,1},{1,0},{2,3},{3,2},{4,5},{5,4},{6,7},{7,6},{8,9},{9,8},{10,11... | collective-permute-start | bytes 1572872 | tf_op jit(solution)/shard_map/ppermute | solution.py:352
  69.1 10.8 %collective-permute-start.15 = (bf16[4,512,128]{2,1,0:T(8,128)(2,1)}, bf16[4,512,128]{2,1,0:T(8,128)(2,1)S(1)}, u32[]{:S(2)}, u32[]{:S(2)}) collective-permute-start(bf16[4,512,128]{2,1,0:T(8,128)(2,1)} %collective-permute-done.11.refs_2_), channel_id=1, source_target_pairs={{0,1},{1,0},{2,3},{3,2},{4,5},{5,4},{6,7},{7,6},{8,9},{9,8},{10,11... | collective-permute-start | bytes 1572872 | tf_op jit(solution)/shard_map/ppermute | solution.py:352
  69.1 10.8 %collective-permute-start.16 = (bf16[4,512,128]{2,1,0:T(8,128)(2,1)}, bf16[4,512,128]{2,1,0:T(8,128)(2,1)S(1)}, u32[]{:S(2)}, u32[]{:S(2)}) collective-permute-start(bf16[4,512,128]{2,1,0:T(8,128)(2,1)} %collective-permute-done.12.refs_3_), channel_id=1, source_target_pairs={{0,1},{1,0},{2,3},{3,2},{4,5},{5,4},{6,7},{7,6},{8,9},{9,8},{10,11... | collective-permute-start | bytes 1572872 | tf_op jit(solution)/shard_map/ppermute | solution.py:352
  69.7 17.7 %collective-permute-start.4 = (bf16[512,256]{1,0:T(8,128)(2,1)S(1)}, bf16[512,256]{1,0:T(8,128)(2,1)S(1)}, u32[]{:S(2)}, u32[]{:S(2)}) collective-permute-start(bf16[512,256]{1,0:T(8,128)(2,1)S(1)} %fusion.4), channel_id=1, source_target_pairs={{0,8},{1,9},{2,10},{3,11},{4,12},{5,13},{6,14},{7,15},{8,16},{9,17... | collective-permute-start | bytes 786440 | tf_op jit(solution)/shard_map/ppermute | solution.py:352
  75.7 20.4 %collective-permute-start.5 = (bf16[512,256]{1,0:T(8,128)(2,1)S(1)}, bf16[512,256]{1,0:T(8,128)(2,1)S(1)}, u32[]{:S(2)}, u32[]{:S(2)}) collective-permute-start(bf16[512,256]{1,0:T(8,128)(2,1)S(1)} %fusion.4), channel_id=1, source_target_pairs={{0,16},{1,17},{2,18},{3,19},{4,20},{5,21},{6,22},{7,23},{8,24},{9,... | collective-permute-start | bytes 786440 | tf_op jit(solution)/shard_map/ppermute | solution.py:352
  78.8 17.3 %collective-permute-start.6 = (bf16[512,256]{1,0:T(8,128)(2,1)S(1)}, bf16[512,256]{1,0:T(8,128)(2,1)S(1)}, u32[]{:S(2)}, u32[]{:S(2)}) collective-permute-start(bf16[512,256]{1,0:T(8,128)(2,1)S(1)} %fusion.4), channel_id=1, source_target_pairs={{0,24},{1,25},{2,26},{3,27},{4,28},{5,29},{6,30},{7,31},{8,0},{9,1... | collective-permute-start | bytes 786440 | tf_op jit(solution)/shard_map/ppermute | solution.py:352
  86.8 9.2 %collective-permute-start.17 = (bf16[256,256]{1,0:T(8,128)(2,1)S(1)}, bf16[256,256]{1,0:T(8,128)(2,1)S(1)}, u32[]{:S(2)}, u32[]{:S(2)}) collective-permute-start(bf16[256,256]{1,0:T(8,128)(2,1)S(1)} %get-tuple-element.71), channel_id=1, source_target_pairs={{0,4},{1,5},{2,6},{3,7},{4,0},{5,1},{6,2},{7,3},{8,12},{9,13},{10,... | collective-permute-start | bytes 393224 | tf_op jit(solution)/shard_map/ppermute | solution.py:352
  97.9 7.6 %collective-permute-start.18 = (bf16[4,512,256]{2,1,0:T(8,128)(2,1)}, bf16[4,512,256]{2,1,0:T(8,128)(2,1)}, u32[]{:S(2)}, u32[]{:S(2)}) collective-permute-start(bf16[4,512,256]{2,1,0:T(8,128)(2,1)} %pad_maximum_fusion.refs_0_), channel_id=1, source_target_pairs={{0,1},{1,0},{2,3},{3,2},{4,5},{5,4},{6,7},{7,6},{8,9},{9,8},{10,11... | collective-permute-start | bytes 3145736 | tf_op jit(solution)/shard_map/ppermute | solution.py:352
  97.9 40.6 %collective-permute-start.19 = (bf16[4,512,256]{2,1,0:T(8,128)(2,1)}, bf16[4,512,256]{2,1,0:T(8,128)(2,1)}, u32[]{:S(2)}, u32[]{:S(2)}) collective-permute-start(bf16[4,512,256]{2,1,0:T(8,128)(2,1)} %pad_maximum_fusion.refs_0_), channel_id=1, source_target_pairs={{0,4},{1,5},{2,6},{3,7},{4,0},{5,1},{6,2},{7,3},{8,12},{9,13},{10,... | collective-permute-start | bytes 3145736 | tf_op jit(solution)/shard_map/ppermute | solution.py:352
  99.3 10.4 %collective-permute-start.22 = (bf16[256,256]{1,0:T(8,128)(2,1)S(1)}, bf16[256,256]{1,0:T(8,128)(2,1)S(1)}, u32[]{:S(2)}, u32[]{:S(2)}) collective-permute-start(bf16[256,256]{1,0:T(8,128)(2,1)S(1)} %add_convert_fusion.3.refs_9_), channel_id=1, source_target_pairs={{0,8},{1,9},{2,10},{3,11},{4,12},{5,13},{6,14},{7,15},{8,16},{9,17... | collective-permute-start | bytes 393224 | tf_op jit(solution)/shard_map/ppermute | solution.py:352
  107.6 30.9 %collective-permute-start.20 = (bf16[2,512,256]{2,1,0:T(8,128)(2,1)}, bf16[2,512,256]{2,1,0:T(8,128)(2,1)}, u32[]{:S(2)}, u32[]{:S(2)}) collective-permute-start(bf16[2,512,256]{2,1,0:T(8,128)(2,1)} %dynamic-slice_select_fusion), channel_id=1, source_target_pairs={{0,2},{1,3},{2,0},{3,1},{4,6},{5,7},{6,4},{7,5},{8,10},{9,11},{10,... | collective-permute-start | bytes 1572872 | tf_op jit(solution)/shard_map/ppermute | solution.py:352
  109.1 29.3 %collective-permute-start.21 = (bf16[2,512,256]{2,1,0:T(8,128)(2,1)}, bf16[2,512,256]{2,1,0:T(8,128)(2,1)}, u32[]{:S(2)}, u32[]{:S(2)}) collective-permute-start(bf16[2,512,256]{2,1,0:T(8,128)(2,1)} %dynamic-slice_select_fusion), channel_id=1, source_target_pairs={{0,3},{1,2},{2,1},{3,0},{4,7},{5,6},{6,5},{7,4},{8,11},{9,10},{10,... | collective-permute-start | bytes 1572872 | tf_op jit(solution)/shard_map/ppermute | solution.py:352
  109.3 29.2 %collective-permute-start.23 = (bf16[256,256]{1,0:T(8,128)(2,1)S(1)}, bf16[256,256]{1,0:T(8,128)(2,1)S(1)}, u32[]{:S(2)}, u32[]{:S(2)}) collective-permute-start(bf16[256,256]{1,0:T(8,128)(2,1)S(1)} %add_convert_fusion.3.refs_9_), channel_id=1, source_target_pairs={{0,16},{1,17},{2,18},{3,19},{4,20},{5,21},{6,22},{7,23},{8,24},{9,... | collective-permute-start | bytes 393224 | tf_op jit(solution)/shard_map/ppermute | solution.py:352
  109.7 28.7 %collective-permute-start.24 = (bf16[256,256]{1,0:T(8,128)(2,1)S(1)}, bf16[256,256]{1,0:T(8,128)(2,1)S(1)}, u32[]{:S(2)}, u32[]{:S(2)}) collective-permute-start(bf16[256,256]{1,0:T(8,128)(2,1)S(1)} %add_convert_fusion.3.refs_9_), channel_id=1, source_target_pairs={{0,24},{1,25},{2,26},{3,27},{4,28},{5,29},{6,30},{7,31},{8,0},{9,1... | collective-permute-start | bytes 393224 | tf_op jit(solution)/shard_map/ppermute | solution.py:352
  113.1 25.3 %copy-start.3 = (f32[2048,256]{1,0:T(8,128)S(1)}, f32[2048,256]{1,0:T(8,128)}, u32[]{:S(2)}) copy-start(f32[2048,256]{1,0:T(8,128)} %refs_7_.1) | copy-start | bytes 6291460
  146.8 1.2 collective-permute-start.25
  148.0 3.6 %collective-permute-start.26 = (f32[4,256]{1,0:T(4,128)S(1)}, f32[4,256]{1,0:T(4,128)S(1)}, u32[]{:S(2)}, u32[]{:S(2)}) collective-permute-start(f32[4,256]{1,0:T(4,128)S(1)} %add.207), channel_id=1, source_target_pairs={{0,2},{1,3},{2,0},{3,1},{4,6},{5,7},{6,4},{7,5},{8,10},{9,11},{10,... | collective-permute-start | bytes 12296 | tf_op jit(solution)/shard_map/ppermute | solution.py:352
  151.6 3.6 %collective-permute-start.27 = (f32[4,256]{1,0:T(4,128)S(1)}, f32[4,256]{1,0:T(4,128)S(1)}, u32[]{:S(2)}, u32[]{:S(2)}) collective-permute-start(f32[4,256]{1,0:T(4,128)S(1)} %add.208), channel_id=1, source_target_pairs={{0,4},{1,5},{2,6},{3,7},{4,0},{5,1},{6,2},{7,3},{8,12},{9,13},{10,... | collective-permute-start | bytes 12296 | tf_op jit(solution)/shard_map/ppermute | solution.py:352
  155.2 5.4 %collective-permute-start.28 = (f32[4,256]{1,0:T(4,128)S(1)}, f32[4,256]{1,0:T(4,128)S(1)}, u32[]{:S(2)}, u32[]{:S(2)}) collective-permute-start(f32[4,256]{1,0:T(4,128)S(1)} %add.209), channel_id=1, source_target_pairs={{0,8},{1,9},{2,10},{3,11},{4,12},{5,13},{6,14},{7,15},{8,16},{9,17... | collective-permute-start | bytes 12296 | tf_op jit(solution)/shard_map/ppermute | solution.py:352
  155.2 5.4 %collective-permute-start.29 = (f32[4,256]{1,0:T(4,128)S(1)}, f32[4,256]{1,0:T(4,128)S(1)}, u32[]{:S(2)}, u32[]{:S(2)}) collective-permute-start(f32[4,256]{1,0:T(4,128)S(1)} %add.209), channel_id=1, source_target_pairs={{0,16},{1,17},{2,18},{3,19},{4,20},{5,21},{6,22},{7,23},{8,24},{9,... | collective-permute-start | bytes 12296 | tf_op jit(solution)/shard_map/ppermute | solution.py:352
  155.5 5.7 %collective-permute-start.30 = (f32[4,256]{1,0:T(4,128)S(1)}, f32[4,256]{1,0:T(4,128)S(1)}, u32[]{:S(2)}, u32[]{:S(2)}) collective-permute-start(f32[4,256]{1,0:T(4,128)S(1)} %add.209), channel_id=1, source_target_pairs={{0,24},{1,25},{2,26},{3,27},{4,28},{5,29},{6,30},{7,31},{8,0},{9,1... | collective-permute-start | bytes 12296 | tf_op jit(solution)/shard_map/ppermute | solution.py:352
  (10 other events, 69.9 us)

commit v2 on v1

--- a/solution.py
+++ b/solution.py
@@ -462,11 +462,15 @@
         after(plan, gram_new), stacked, other, found, grads_col, grads_row, sums, queries,
         [copy], scale, 1.0 / col_count,
     )
-    sums = sums + swap_core(sums)
-    bit = 1
-    while bit < files:
-        sums = sums + flip_x(sums, bit)
-        bit *= 2
+    if files == 2:
+        across = move(sums, lambda z, y, x, k: (z, y, x ^ 1, 1 - k))
+        sums = (sums + swap_core(sums)) + (flip_x(sums, 1) + across)
+    else:
+        sums = sums + swap_core(sums)
+        bit = 1
+        while bit < files:
+            sums = sums + flip_x(sums, bit)
+            bit *= 2
     sums = sums + swap_y(sums)
     around = jnp.stack(spread_z(sums))
     sums = sum(

time: 166 us -> 165 us (level)
  waiting for transfers between devices: 41.5 us -> 39.3 us
    ppermute x31 -> x32, waiting for transfers between devices: 41.5 us -> 39.3 us  [move(): return lax.ppermute(value, ('row', 'col'), pairs)]
    ppermute x31 -> x32, starting transfers between devices: 46.6 us -> 47.8 us  [move(): return lax.ppermute(value, ('row', 'col'), pairs)]
  transfers between devices with their start and end apart: 31 -> 32, of which waited for: 11 -> 11; matrix products, arithmetic and copies ran while one was open for 7% -> 7% of each run, Pallas kernels for 24% -> 24%
where the time goes in v2:
time: 165 us; the launch traced here: 164 us
  Pallas kernels  56 us (34%)
  starting transfers between devices  47.8 us (29%)
  waiting for transfers between devices  39.3 us (24%)
  other arithmetic  12.6 us (8%)
  local copies, waits for them, and re-layouts  4.25 us (3%)
  matrix products  3.38 us (2%)
    ppermute x32, starting transfers between devices, move(): return lax.ppermute(value, ('row', 'col'), pairs)  47.8 us
    ppermute x32, waiting for transfers between devices, move(): return lax.ppermute(value, ('row', 'col'), pairs)  39.3 us
    pallas_call x1, Pallas kernels, update_gram(): pl.pallas_call(functools.partial(gram_kernel, scale, block, first), grid_...  25.3 us
    pallas_call x2, Pallas kernels, back_product(): pl.pallas_call(functools.partial(back_kernel, streams), grid_spec=pltpu.P...  17.3 us
    pallas_call x1, Pallas kernels, tail(): pl.pallas_call(functools.partial(tail_kernel, scale, even, len(copies)),...  7.02 us
    pallas_call x1, Pallas kernels, build_grads(): pl.pallas_call(functools.partial(grads_kernel, parts, cols // rank, rows...  6.39 us
    sub x1, other arithmetic, shards(): (step + step_next * (1.0 + momentum)) * queries - step_next * step * mapped  3.97 us
    unnamed x23, local copies, waits for them, and re-layouts  3.93 us
  transfers between devices with their start and end apart: 32, of which 11 were waited for; matrix products, arithmetic and copies ran while one was open for 7% of the time, Pallas kernels for 24%

profile of v2, /device:TPU:0, one launch (start us, length us, event | category | flops | bytes accessed | tf_op | source)
XLA Modules:
  0.0 164.3 jit_solution(17771236904313745653)
XLA Ops:
  0.7 1.9 %copy.10 = bf16[2048,256]{0,1:T(8,128)(2,1)S(1)} copy(f32[2048,256]{1,0:T(8,128)} %refs_7_.1) | data formatting | bytes 3145728 | tf_op args[6]
  2.7 9.1 %back_product.2 = bf16[2048,256]{1,0:T(8,128)(2,1)} custom-call(s32[2]{0:T(128)S(1)} %get-tuple-element.74.plan_ref, bf16[256,2048]{1,0:T(8,128)(2,1)S(1)} %bitcast.105, f32[2048,4096]{1,0:T(8,128)} %gram_ref.1, f32[2048,4096]{1,0:T(8,128)} %gram_ref.1), custom_call_target="tpu_custom_call" | custom-call | flops 2147483648 | bytes 18874368 | tf_op jit(solution)/shard_map/back_product/pallas_call | solution.py:142
  11.7 3.0 %collective-permute-start = (bf16[2048,256]{1,0:T(8,128)(2,1)}, bf16[2048,256]{1,0:T(8,128)(2,1)}, u32[]{:S(2)}, u32[]{:S(2)}) collective-permute-start(bf16[2048,256]{1,0:T(8,128)(2,1)} %back_product.2), channel_id=1, source_target_pairs={{0,4},{1,5},{2,6},{3,7},{4,0},{5,1},{6,2},{7,3},{8,12},{9,13},{10,... | collective-permute-start | bytes 3145736 | tf_op jit(solution)/shard_map/ppermute | solution.py:352
  14.9 2.2 %fusion.1 = bf16[16,2,8,128]{3,2,1,0:T(8,128)(2,1)S(1)} fusion(bf16[4096,128]{1,0:T(8,128)(2,1)} %param.10, bf16[256,4096]{1,0:T(8,128)(2,1)S(1)} %copy-done, pred[256]{0:T(512)(128)(4,1)S(1)} %fusion.10), kind=kOutput, calls=%fused_computation.4 | convolution fusion | flops 268500992 | bytes 3211520 | tf_op jit(solution)/shard_map/dot_general | solution.py:21
  17.9 1.6 collective-permute-start.7
  19.5 2.6 %collective-permute-start.8 = (bf16[512,128]{1,0:T(8,128)(2,1)S(1)}, bf16[512,128]{1,0:T(8,128)(2,1)S(1)}, u32[]{:S(2)}, u32[]{:S(2)}) collective-permute-start(bf16[512,128]{1,0:T(8,128)(2,1)S(1)} %pad_maximum_fusion.2), channel_id=1, source_target_pairs={{0,16},{1,17},{2,18},{3,19},{4,20},{5,21},{6,22},{7,23},{8,24},{9,... | collective-permute-start | bytes 393224 | tf_op jit(solution)/shard_map/ppermute | solution.py:352
  23.4 8.2 %back_product.3 = f32[2048,256]{1,0:T(8,128)S(1)} custom-call(s32[2]{0:T(128)S(1)} %get-tuple-element.34.plan_ref, bf16[256,2048]{1,0:T(8,128)(2,1)S(1)} %bitcast.106, f32[2048,4096]{1,0:T(8,128)} %gram_ref.1, f32[2048,4096]{1,0:T(8,128)} %gram_ref.1, f32[2048,256]{1,0:T(8,128)S(1)} %copy-done.2), custom_call_target="tpu_custom_call" | custom-call | flops 2147483648 | bytes 18874368 | tf_op jit(solution)/shard_map/back_product/pallas_call | solution.py:142
  32.6 1.5 collective-permute-start.11
  34.0 4.1 %collective-permute-done = bf16[2048,256]{1,0:T(8,128)(2,1)} collective-permute-done((bf16[2048,256]{1,0:T(8,128)(2,1)}, bf16[2048,256]{1,0:T(8,128)(2,1)}, u32[]{:S(2)}, u32[]{:S(2)}) %collective-permute-start) | collective-permute-done | bytes 1048608 | tf_op jit(solution)/shard_map/ppermute | solution.py:352
  38.2 2.1 %fusion.7 = (bf16[512,256]{1,0:T(8,128)(2,1)}, bf16[512,256]{1,0:T(8,128)(2,1)S(1)}, bf16[512,256]{1,0:T(8,128)(2,1)}) fusion(f32[4,512,256]{2,1,0:T(8,128)S(1)} %bitcast.107, s32[]{:T(128)S(6)} %select_n.130, bf16[4,512,256]{2,1,0:T(8,128)(2,1)} %bitcast.13, s32[]{:T(128)S(6)} %select_n.134, s32[]{:T(128)S(6)} %select_n.132), kind=kLoop, calls=%fused_computation.18 | loop fusion | flops 1179648 | bytes 3145740 | tf_op jit(solution)/shard_map/convert_element_type | solution.py:395
  40.3 5.2 %collective-permute-done.11.refs_2_ = bf16[4,512,128]{2,1,0:T(8,128)(2,1)} collective-permute-done((bf16[4,512,128]{2,1,0:T(8,128)(2,1)}, bf16[4,512,128]{2,1,0:T(8,128)(2,1)}, u32[]{:S(2)}, u32[]{:S(2)}) %collective-permute-start.11) | collective-permute-done | bytes 524320 | tf_op jit(solution)/shard_map/ppermute | solution.py:352
  45.9 1.5 collective-permute-start.10
  47.5 3.5 %collective-permute-start.1 = (bf16[512,256]{1,0:T(8,128)(2,1)}, bf16[512,256]{1,0:T(8,128)(2,1)}, u32[]{:S(2)}, u32[]{:S(2)}) collective-permute-start(bf16[512,256]{1,0:T(8,128)(2,1)} %get-tuple-element.68), channel_id=1, source_target_pairs={{0,8},{1,9},{2,10},{3,11},{4,12},{5,13},{6,14},{7,15},{8,16},{9,17... | collective-permute-start | bytes 786440 | tf_op jit(solution)/shard_map/ppermute | solution.py:352
  50.9 2.4 %collective-permute-start.3 = (bf16[512,256]{1,0:T(8,128)(2,1)S(1)}, bf16[512,256]{1,0:T(8,128)(2,1)}, u32[]{:S(2)}, u32[]{:S(2)}) collective-permute-start(bf16[512,256]{1,0:T(8,128)(2,1)S(1)} %get-tuple-element.69), channel_id=1, source_target_pairs={{0,24},{1,25},{2,26},{3,27},{4,28},{5,29},{6,30},{7,31},{8,0},{9,1... | collective-permute-start | bytes 786440 | tf_op jit(solution)/shard_map/ppermute | solution.py:352
  53.3 5.5 %collective-permute-done.1 = bf16[512,256]{1,0:T(8,128)(2,1)} collective-permute-done((bf16[512,256]{1,0:T(8,128)(2,1)}, bf16[512,256]{1,0:T(8,128)(2,1)}, u32[]{:S(2)}, u32[]{:S(2)}) %collective-permute-start.1) | collective-permute-done | bytes 262176 | tf_op jit(solution)/shard_map/ppermute | solution.py:352
  58.8 8.2 %collective-permute-done.2 = bf16[512,256]{1,0:T(8,128)(2,1)} collective-permute-done((bf16[512,256]{1,0:T(8,128)(2,1)}, bf16[512,256]{1,0:T(8,128)(2,1)}, u32[]{:S(2)}, u32[]{:S(2)}) %collective-permute-start.2) | collective-permute-done | bytes 262176 | tf_op jit(solution)/shard_map/ppermute | solution.py:352
  69.7 5.9 %collective-permute-start.4 = (bf16[512,256]{1,0:T(8,128)(2,1)S(1)}, bf16[512,256]{1,0:T(8,128)(2,1)S(1)}, u32[]{:S(2)}, u32[]{:S(2)}) collective-permute-start(bf16[512,256]{1,0:T(8,128)(2,1)S(1)} %fusion.4), channel_id=1, source_target_pairs={{0,8},{1,9},{2,10},{3,11},{4,12},{5,13},{6,14},{7,15},{8,16},{9,17... | collective-permute-start | bytes 786440 | tf_op jit(solution)/shard_map/ppermute | solution.py:352
  75.7 3.1 %collective-permute-start.5 = (bf16[512,256]{1,0:T(8,128)(2,1)S(1)}, bf16[512,256]{1,0:T(8,128)(2,1)S(1)}, u32[]{:S(2)}, u32[]{:S(2)}) collective-permute-start(bf16[512,256]{1,0:T(8,128)(2,1)S(1)} %fusion.4), channel_id=1, source_target_pairs={{0,16},{1,17},{2,18},{3,19},{4,20},{5,21},{6,22},{7,23},{8,24},{9,... | collective-permute-start | bytes 786440 | tf_op jit(solution)/shard_map/ppermute | solution.py:352
  80.0 6.4 %build_grads.1 = (bf16[256,4096]{1,0:T(8,128)(2,1)S(1)}, bf16[256,2048]{1,0:T(8,128)(2,1)S(1)}) custom-call(s32[2]{0:T(128)S(1)} %pad_add_fusion.2.at_ref, bf16[4,512,128]{2,1,0:T(8,128)(2,1)} %pad_maximum_fusion.1.refs_0_, bf16[4,512,128]{2,1,0:T(8,128)(2,1)} %collective-permute-done.10.refs_1_, bf16[4,512,128]{2,1,0:T(8,128)(2,1)} %collective-permute-done.11.refs_2_, ...), custom_call_target="tpu_custom_call" | custom-call | flops 805306368 | bytes 3145728 | tf_op jit(solution)/shard_map/build_grads/pallas_call | solution.py:88
  87.4 8.7 %collective-permute-done.5 = bf16[512,256]{1,0:T(8,128)(2,1)S(1)} collective-permute-done((bf16[512,256]{1,0:T(8,128)(2,1)S(1)}, bf16[512,256]{1,0:T(8,128)(2,1)S(1)}, u32[]{:S(2)}, u32[]{:S(2)}) %collective-permute-start.5) | collective-permute-done | bytes 262176 | tf_op jit(solution)/shard_map/ppermute | solution.py:352
  99.3 6.1 %collective-permute-start.22 = (bf16[256,256]{1,0:T(8,128)(2,1)S(1)}, bf16[256,256]{1,0:T(8,128)(2,1)S(1)}, u32[]{:S(2)}, u32[]{:S(2)}) collective-permute-start(bf16[256,256]{1,0:T(8,128)(2,1)S(1)} %add_convert_fusion.3.refs_9_), channel_id=1, source_target_pairs={{0,8},{1,9},{2,10},{3,11},{4,12},{5,13},{6,14},{7,15},{8,16},{9,17... | collective-permute-start | bytes 393224 | tf_op jit(solution)/shard_map/ppermute | solution.py:352
  105.5 2.1 %dynamic-slice_select_fusion = bf16[2,512,256]{2,1,0:T(8,128)(2,1)} fusion(bf16[4,512,256]{2,1,0:T(8,128)(2,1)} %collective-permute-done.18.refs_2_, s32[]{:T(128)S(6)} %select_n.136, bf16[4,512,256]{2,1,0:T(8,128)(2,1)} %pad_maximum_fusion.refs_0_, pred[]{:T(512)S(6)} %eq.29), kind=kLoop, calls=%fused_computation.6 | loop fusion | flops 262144 | bytes 1572869 | tf_op jit(solution)/shard_map/jit(_where)/select_n | solution.py:428
  107.6 1.5 collective-permute-start.20
  109.7 3.4 %collective-permute-start.24 = (bf16[256,256]{1,0:T(8,128)(2,1)S(1)}, bf16[256,256]{1,0:T(8,128)(2,1)S(1)}, u32[]{:S(2)}, u32[]{:S(2)}) collective-permute-start(bf16[256,256]{1,0:T(8,128)(2,1)S(1)} %add_convert_fusion.3.refs_9_), channel_id=1, source_target_pairs={{0,24},{1,25},{2,26},{3,27},{4,28},{5,29},{6,30},{7,31},{8,0},{9,1... | collective-permute-start | bytes 393224 | tf_op jit(solution)/shard_map/ppermute | solution.py:352
  113.1 25.3 %update_gram.1 = (f32[2048,4096]{1,0:T(8,128)}, bf16[2048,3072]{1,0:T(8,128)(2,1)S(1)}) custom-call(s32[7]{0:T(128)S(1)} %stack.128.at_ref, f32[2048,4096]{1,0:T(8,128)} %gram_ref.1, bf16[256,2048]{1,0:T(8,128)(2,1)S(1)} %copy-done.5, bf16[256,4096]{1,0:T(8,128)(2,1)S(1)} %get-tuple-element.51.right_ref.refs_5_), custom_call_target="tpu_custom_call" | custom-call | flops 4294967296 | bytes 67108864 | tf_op jit(solution)/shard_map/update_gram/pallas_call | solution.py:201
  138.5 7.0 %tail.1 = (f32[2048,256]{1,0:T(8,128)S(1)}, f32[4,256]{1,0:T(4,128)S(1)}) custom-call(s32[9]{0:T(128)S(1)} %concatenate.7.plan_ref, bf16[4,512,256]{2,1,0:T(8,128)(2,1)} %pad_maximum_fusion.refs_0_, bf16[4,512,256]{2,1,0:T(8,128)(2,1)} %collective-permute-done.19.refs_1_, bf16[4,512,256]{2,1,0:T(8,128)(2,1)} %collective-permute-done.18.refs_2_, ...), custom_call_target="tpu_custom_call" | custom-call | flops 4294967296 | bytes 16777216 | tf_op jit(solution)/shard_map/tail/pallas_call | solution.py:299
  148.7 1.7 %collective-permute-done.26 = f32[4,256]{1,0:T(4,128)S(1)} collective-permute-done((f32[4,256]{1,0:T(4,128)S(1)}, f32[4,256]{1,0:T(4,128)S(1)}, u32[]{:S(2)}, u32[]{:S(2)}) %collective-permute-start.26) | collective-permute-done | bytes 4128 | tf_op jit(solution)/shard_map/ppermute | solution.py:352
  151.1 3.2 %collective-permute-done.28 = f32[4,256]{1,0:T(4,128)S(1)} collective-permute-done((f32[4,256]{1,0:T(4,128)S(1)}, f32[4,256]{1,0:T(4,128)S(1)}, u32[]{:S(2)}, u32[]{:S(2)}) %collective-permute-start.28) | collective-permute-done | bytes 4128 | tf_op jit(solution)/shard_map/ppermute | solution.py:352
  154.2 1.9 %collective-permute-start.30 = (f32[4,256]{1,0:T(4,128)S(1)}, f32[4,256]{1,0:T(4,128)S(1)}, u32[]{:S(2)}, u32[]{:S(2)}) collective-permute-start(f32[4,256]{1,0:T(4,128)S(1)} %add.213), channel_id=1, source_target_pairs={{0,16},{1,17},{2,18},{3,19},{4,20},{5,21},{6,22},{7,23},{8,24},{9,... | collective-permute-start | bytes 12296 | tf_op jit(solution)/shard_map/ppermute | solution.py:352
  156.1 1.9 %collective-permute-start.31 = (f32[4,256]{1,0:T(4,128)S(1)}, f32[4,256]{1,0:T(4,128)S(1)}, u32[]{:S(2)}, u32[]{:S(2)}) collective-permute-start(f32[4,256]{1,0:T(4,128)S(1)} %add.213), channel_id=1, source_target_pairs={{0,24},{1,25},{2,26},{3,27},{4,28},{5,29},{6,30},{7,31},{8,0},{9,1... | collective-permute-start | bytes 12296 | tf_op jit(solution)/shard_map/ppermute | solution.py:352
  158.1 1.6 collective-permute-done.29
  160.3 4.0 %multiply_subtract_fusion = f32[2048,256]{1,0:T(8,128)} fusion(f32[2048,256]{1,0:T(8,128)} %copy-done.6, f32[2048,256]{1,0:T(8,128)} %refs_7_.1, f32[256]{0:T(256)S(1)} %bitcast.119, f32[256]{0:T(256)S(1)} %bitcast.120), kind=kLoop, calls=%fused_computation | loop fusion | flops 1572864 | bytes 6293504 | tf_op jit(solution)/shard_map/sub | solution.py:485
  (86 shorter events, 16.9 us)
Async XLA Ops:
  11.7 26.4 %collective-permute-start = (bf16[2048,256]{1,0:T(8,128)(2,1)}, bf16[2048,256]{1,0:T(8,128)(2,1)}, u32[]{:S(2)}, u32[]{:S(2)}) collective-permute-start(bf16[2048,256]{1,0:T(8,128)(2,1)} %back_product.2), channel_id=1, source_target_pairs={{0,4},{1,5},{2,6},{3,7},{4,0},{5,1},{6,2},{7,3},{8,12},{9,13},{10,... | collective-permute-start | bytes 3145736 | tf_op jit(solution)/shard_map/ppermute | solution.py:352
  17.9 13.8 %collective-permute-start.7 = (bf16[512,128]{1,0:T(8,128)(2,1)S(1)}, bf16[512,128]{1,0:T(8,128)(2,1)S(1)}, u32[]{:S(2)}, u32[]{:S(2)}) collective-permute-start(bf16[512,128]{1,0:T(8,128)(2,1)S(1)} %pad_maximum_fusion.2), channel_id=1, source_target_pairs={{0,8},{1,9},{2,10},{3,11},{4,12},{5,13},{6,14},{7,15},{8,16},{9,17... | collective-permute-start | bytes 393224 | tf_op jit(solution)/shard_map/ppermute | solution.py:352
  19.5 12.2 %collective-permute-start.8 = (bf16[512,128]{1,0:T(8,128)(2,1)S(1)}, bf16[512,128]{1,0:T(8,128)(2,1)S(1)}, u32[]{:S(2)}, u32[]{:S(2)}) collective-permute-start(bf16[512,128]{1,0:T(8,128)(2,1)S(1)} %pad_maximum_fusion.2), channel_id=1, source_target_pairs={{0,16},{1,17},{2,18},{3,19},{4,20},{5,21},{6,22},{7,23},{8,24},{9,... | collective-permute-start | bytes 393224 | tf_op jit(solution)/shard_map/ppermute | solution.py:352
  22.1 9.6 %collective-permute-start.9 = (bf16[512,128]{1,0:T(8,128)(2,1)S(1)}, bf16[512,128]{1,0:T(8,128)(2,1)S(1)}, u32[]{:S(2)}, u32[]{:S(2)}) collective-permute-start(bf16[512,128]{1,0:T(8,128)(2,1)S(1)} %pad_maximum_fusion.2), channel_id=1, source_target_pairs={{0,24},{1,25},{2,26},{3,27},{4,28},{5,29},{6,30},{7,31},{8,0},{9,1... | collective-permute-start | bytes 393224 | tf_op jit(solution)/shard_map/ppermute | solution.py:352
  32.6 12.9 %collective-permute-start.11 = (bf16[4,512,128]{2,1,0:T(8,128)(2,1)}, bf16[4,512,128]{2,1,0:T(8,128)(2,1)}, u32[]{:S(2)}, u32[]{:S(2)}) collective-permute-start(bf16[4,512,128]{2,1,0:T(8,128)(2,1)} %pad_maximum_fusion.1.refs_0_), channel_id=1, source_target_pairs={{0,2},{1,3},{2,0},{3,1},{4,6},{5,7},{6,4},{7,5},{8,10},{9,11},{10,... | collective-permute-start | bytes 1572872 | tf_op jit(solution)/shard_map/ppermute | solution.py:352
  45.4 23.0 %collective-permute-start.12 = (bf16[4,512,128]{2,1,0:T(8,128)(2,1)}, bf16[4,512,128]{2,1,0:T(8,128)(2,1)}, u32[]{:S(2)}, u32[]{:S(2)}) collective-permute-start(bf16[4,512,128]{2,1,0:T(8,128)(2,1)} %collective-permute-done.11.refs_2_), channel_id=1, source_target_pairs={{0,4},{1,5},{2,6},{3,7},{4,0},{5,1},{6,2},{7,3},{8,12},{9,13},{10,... | collective-permute-start | bytes 1572872 | tf_op jit(solution)/shard_map/ppermute | solution.py:352
  45.9 22.7 %collective-permute-start.10 = (bf16[4,512,128]{2,1,0:T(8,128)(2,1)}, bf16[4,512,128]{2,1,0:T(8,128)(2,1)}, u32[]{:S(2)}, u32[]{:S(2)}) collective-permute-start(bf16[4,512,128]{2,1,0:T(8,128)(2,1)} %pad_maximum_fusion.1.refs_0_), channel_id=1, source_target_pairs={{0,4},{1,5},{2,6},{3,7},{4,0},{5,1},{6,2},{7,3},{8,12},{9,13},{10,... | collective-permute-start | bytes 1572872 | tf_op jit(solution)/shard_map/ppermute | solution.py:352
  47.5 11.4 %collective-permute-start.1 = (bf16[512,256]{1,0:T(8,128)(2,1)}, bf16[512,256]{1,0:T(8,128)(2,1)}, u32[]{:S(2)}, u32[]{:S(2)}) collective-permute-start(bf16[512,256]{1,0:T(8,128)(2,1)} %get-tuple-element.68), channel_id=1, source_target_pairs={{0,8},{1,9},{2,10},{3,11},{4,12},{5,13},{6,14},{7,15},{8,16},{9,17... | collective-permute-start | bytes 786440 | tf_op jit(solution)/shard_map/ppermute | solution.py:352
  50.9 16.1 %collective-permute-start.2 = (bf16[512,256]{1,0:T(8,128)(2,1)}, bf16[512,256]{1,0:T(8,128)(2,1)}, u32[]{:S(2)}, u32[]{:S(2)}) collective-permute-start(bf16[512,256]{1,0:T(8,128)(2,1)} %get-tuple-element.70), channel_id=1, source_target_pairs={{0,16},{1,17},{2,18},{3,19},{4,20},{5,21},{6,22},{7,23},{8,24},{9,... | collective-permute-start | bytes 786440 | tf_op jit(solution)/shard_map/ppermute | solution.py:352
  50.9 16.1 %collective-permute-start.3 = (bf16[512,256]{1,0:T(8,128)(2,1)S(1)}, bf16[512,256]{1,0:T(8,128)(2,1)}, u32[]{:S(2)}, u32[]{:S(2)}) collective-permute-start(bf16[512,256]{1,0:T(8,128)(2,1)S(1)} %get-tuple-element.69), channel_id=1, source_target_pairs={{0,24},{1,25},{2,26},{3,27},{4,28},{5,29},{6,30},{7,31},{8,0},{9,1... | collective-permute-start | bytes 786440 | tf_op jit(solution)/shard_map/ppermute | solution.py:352
  68.6 7.0 %collective-permute-start.13 = (bf16[4,512,128]{2,1,0:T(8,128)(2,1)}, bf16[4,512,128]{2,1,0:T(8,128)(2,1)S(1)}, u32[]{:S(2)}, u32[]{:S(2)}) collective-permute-start(bf16[4,512,128]{2,1,0:T(8,128)(2,1)} %pad_maximum_fusion.1.refs_0_), channel_id=1, source_target_pairs={{0,1},{1,0},{2,3},{3,2},{4,5},{5,4},{6,7},{7,6},{8,9},{9,8},{10,11... | collective-permute-start | bytes 1572872 | tf_op jit(solution)/shard_map/ppermute | solution.py:352
  68.6 10.1 %collective-permute-start.14 = (bf16[4,512,128]{2,1,0:T(8,128)(2,1)}, bf16[4,512,128]{2,1,0:T(8,128)(2,1)S(1)}, u32[]{:S(2)}, u32[]{:S(2)}) collective-permute-start(bf16[4,512,128]{2,1,0:T(8,128)(2,1)} %collective-permute-done.10.refs_1_), channel_id=1, source_target_pairs={{0,1},{1,0},{2,3},{3,2},{4,5},{5,4},{6,7},{7,6},{8,9},{9,8},{10,11... | collective-permute-start | bytes 1572872 | tf_op jit(solution)/shard_map/ppermute | solution.py:352
  69.1 10.8 %collective-permute-start.15 = (bf16[4,512,128]{2,1,0:T(8,128)(2,1)}, bf16[4,512,128]{2,1,0:T(8,128)(2,1)S(1)}, u32[]{:S(2)}, u32[]{:S(2)}) collective-permute-start(bf16[4,512,128]{2,1,0:T(8,128)(2,1)} %collective-permute-done.11.refs_2_), channel_id=1, source_target_pairs={{0,1},{1,0},{2,3},{3,2},{4,5},{5,4},{6,7},{7,6},{8,9},{9,8},{10,11... | collective-permute-start | bytes 1572872 | tf_op jit(solution)/shard_map/ppermute | solution.py:352
  69.1 10.8 %collective-permute-start.16 = (bf16[4,512,128]{2,1,0:T(8,128)(2,1)}, bf16[4,512,128]{2,1,0:T(8,128)(2,1)S(1)}, u32[]{:S(2)}, u32[]{:S(2)}) collective-permute-start(bf16[4,512,128]{2,1,0:T(8,128)(2,1)} %collective-permute-done.12.refs_3_), channel_id=1, source_target_pairs={{0,1},{1,0},{2,3},{3,2},{4,5},{5,4},{6,7},{7,6},{8,9},{9,8},{10,11... | collective-permute-start | bytes 1572872 | tf_op jit(solution)/shard_map/ppermute | solution.py:352
  69.7 17.7 %collective-permute-start.4 = (bf16[512,256]{1,0:T(8,128)(2,1)S(1)}, bf16[512,256]{1,0:T(8,128)(2,1)S(1)}, u32[]{:S(2)}, u32[]{:S(2)}) collective-permute-start(bf16[512,256]{1,0:T(8,128)(2,1)S(1)} %fusion.4), channel_id=1, source_target_pairs={{0,8},{1,9},{2,10},{3,11},{4,12},{5,13},{6,14},{7,15},{8,16},{9,17... | collective-permute-start | bytes 786440 | tf_op jit(solution)/shard_map/ppermute | solution.py:352
  75.7 20.4 %collective-permute-start.5 = (bf16[512,256]{1,0:T(8,128)(2,1)S(1)}, bf16[512,256]{1,0:T(8,128)(2,1)S(1)}, u32[]{:S(2)}, u32[]{:S(2)}) collective-permute-start(bf16[512,256]{1,0:T(8,128)(2,1)S(1)} %fusion.4), channel_id=1, source_target_pairs={{0,16},{1,17},{2,18},{3,19},{4,20},{5,21},{6,22},{7,23},{8,24},{9,... | collective-permute-start | bytes 786440 | tf_op jit(solution)/shard_map/ppermute | solution.py:352
  78.8 17.3 %collective-permute-start.6 = (bf16[512,256]{1,0:T(8,128)(2,1)S(1)}, bf16[512,256]{1,0:T(8,128)(2,1)S(1)}, u32[]{:S(2)}, u32[]{:S(2)}) collective-permute-start(bf16[512,256]{1,0:T(8,128)(2,1)S(1)} %fusion.4), channel_id=1, source_target_pairs={{0,24},{1,25},{2,26},{3,27},{4,28},{5,29},{6,30},{7,31},{8,0},{9,1... | collective-permute-start | bytes 786440 | tf_op jit(solution)/shard_map/ppermute | solution.py:352
  86.8 9.2 %collective-permute-start.17 = (bf16[256,256]{1,0:T(8,128)(2,1)S(1)}, bf16[256,256]{1,0:T(8,128)(2,1)S(1)}, u32[]{:S(2)}, u32[]{:S(2)}) collective-permute-start(bf16[256,256]{1,0:T(8,128)(2,1)S(1)} %get-tuple-element.71), channel_id=1, source_target_pairs={{0,4},{1,5},{2,6},{3,7},{4,0},{5,1},{6,2},{7,3},{8,12},{9,13},{10,... | collective-permute-start | bytes 393224 | tf_op jit(solution)/shard_map/ppermute | solution.py:352
  97.9 7.6 %collective-permute-start.18 = (bf16[4,512,256]{2,1,0:T(8,128)(2,1)}, bf16[4,512,256]{2,1,0:T(8,128)(2,1)}, u32[]{:S(2)}, u32[]{:S(2)}) collective-permute-start(bf16[4,512,256]{2,1,0:T(8,128)(2,1)} %pad_maximum_fusion.refs_0_), channel_id=1, source_target_pairs={{0,1},{1,0},{2,3},{3,2},{4,5},{5,4},{6,7},{7,6},{8,9},{9,8},{10,11... | collective-permute-start | bytes 3145736 | tf_op jit(solution)/shard_map/ppermute | solution.py:352
  97.9 40.6 %collective-permute-start.19 = (bf16[4,512,256]{2,1,0:T(8,128)(2,1)}, bf16[4,512,256]{2,1,0:T(8,128)(2,1)}, u32[]{:S(2)}, u32[]{:S(2)}) collective-permute-start(bf16[4,512,256]{2,1,0:T(8,128)(2,1)} %pad_maximum_fusion.refs_0_), channel_id=1, source_target_pairs={{0,4},{1,5},{2,6},{3,7},{4,0},{5,1},{6,2},{7,3},{8,12},{9,13},{10,... | collective-permute-start | bytes 3145736 | tf_op jit(solution)/shard_map/ppermute | solution.py:352
  99.3 10.4 %collective-permute-start.22 = (bf16[256,256]{1,0:T(8,128)(2,1)S(1)}, bf16[256,256]{1,0:T(8,128)(2,1)S(1)}, u32[]{:S(2)}, u32[]{:S(2)}) collective-permute-start(bf16[256,256]{1,0:T(8,128)(2,1)S(1)} %add_convert_fusion.3.refs_9_), channel_id=1, source_target_pairs={{0,8},{1,9},{2,10},{3,11},{4,12},{5,13},{6,14},{7,15},{8,16},{9,17... | collective-permute-start | bytes 393224 | tf_op jit(solution)/shard_map/ppermute | solution.py:352
  107.6 30.9 %collective-permute-start.20 = (bf16[2,512,256]{2,1,0:T(8,128)(2,1)}, bf16[2,512,256]{2,1,0:T(8,128)(2,1)}, u32[]{:S(2)}, u32[]{:S(2)}) collective-permute-start(bf16[2,512,256]{2,1,0:T(8,128)(2,1)} %dynamic-slice_select_fusion), channel_id=1, source_target_pairs={{0,2},{1,3},{2,0},{3,1},{4,6},{5,7},{6,4},{7,5},{8,10},{9,11},{10,... | collective-permute-start | bytes 1572872 | tf_op jit(solution)/shard_map/ppermute | solution.py:352
  109.1 29.3 %collective-permute-start.21 = (bf16[2,512,256]{2,1,0:T(8,128)(2,1)}, bf16[2,512,256]{2,1,0:T(8,128)(2,1)}, u32[]{:S(2)}, u32[]{:S(2)}) collective-permute-start(bf16[2,512,256]{2,1,0:T(8,128)(2,1)} %dynamic-slice_select_fusion), channel_id=1, source_target_pairs={{0,3},{1,2},{2,1},{3,0},{4,7},{5,6},{6,5},{7,4},{8,11},{9,10},{10,... | collective-permute-start | bytes 1572872 | tf_op jit(solution)/shard_map/ppermute | solution.py:352
  109.3 29.2 %collective-permute-start.23 = (bf16[256,256]{1,0:T(8,128)(2,1)S(1)}, bf16[256,256]{1,0:T(8,128)(2,1)S(1)}, u32[]{:S(2)}, u32[]{:S(2)}) collective-permute-start(bf16[256,256]{1,0:T(8,128)(2,1)S(1)} %add_convert_fusion.3.refs_9_), channel_id=1, source_target_pairs={{0,16},{1,17},{2,18},{3,19},{4,20},{5,21},{6,22},{7,23},{8,24},{9,... | collective-permute-start | bytes 393224 | tf_op jit(solution)/shard_map/ppermute | solution.py:352
  109.7 28.7 %collective-permute-start.24 = (bf16[256,256]{1,0:T(8,128)(2,1)S(1)}, bf16[256,256]{1,0:T(8,128)(2,1)S(1)}, u32[]{:S(2)}, u32[]{:S(2)}) collective-permute-start(bf16[256,256]{1,0:T(8,128)(2,1)S(1)} %add_convert_fusion.3.refs_9_), channel_id=1, source_target_pairs={{0,24},{1,25},{2,26},{3,27},{4,28},{5,29},{6,30},{7,31},{8,0},{9,1... | collective-permute-start | bytes 393224 | tf_op jit(solution)/shard_map/ppermute | solution.py:352
  146.8 1.9 %collective-permute-start.25 = (f32[4,256]{1,0:T(4,128)S(1)}, f32[4,256]{1,0:T(4,128)S(1)}, u32[]{:S(2)}, u32[]{:S(2)}) collective-permute-start(f32[4,256]{1,0:T(4,128)S(1)} %get-tuple-element.62), channel_id=1, source_target_pairs={{0,1},{1,0},{2,3},{3,2},{4,5},{5,4},{6,7},{7,6},{8,9},{9,8},{10,11... | collective-permute-start | bytes 12296 | tf_op jit(solution)/shard_map/ppermute | solution.py:352
  146.8 3.6 %collective-permute-start.26 = (f32[4,256]{1,0:T(4,128)S(1)}, f32[4,256]{1,0:T(4,128)S(1)}, u32[]{:S(2)}, u32[]{:S(2)}) collective-permute-start(f32[4,256]{1,0:T(4,128)S(1)} %get-tuple-element.62), channel_id=1, source_target_pairs={{0,2},{1,3},{2,0},{3,1},{4,6},{5,7},{6,4},{7,5},{8,10},{9,11},{10,... | collective-permute-start | bytes 12296 | tf_op jit(solution)/shard_map/ppermute | solution.py:352
  147.6 3.0 %collective-permute-start.27 = (f32[4,256]{1,0:T(4,128)S(1)}, f32[4,256]{1,0:T(4,128)S(1)}, u32[]{:S(2)}, u32[]{:S(2)}) collective-permute-start(f32[4,256]{1,0:T(4,128)S(1)} %get-tuple-element.62), channel_id=1, source_target_pairs={{0,3},{1,2},{2,1},{3,0},{4,7},{5,6},{6,5},{7,4},{8,11},{9,10},{10,... | collective-permute-start | bytes 12296 | tf_op jit(solution)/shard_map/ppermute | solution.py:352
  150.6 3.6 %collective-permute-start.28 = (f32[4,256]{1,0:T(4,128)S(1)}, f32[4,256]{1,0:T(4,128)S(1)}, u32[]{:S(2)}, u32[]{:S(2)}) collective-permute-start(f32[4,256]{1,0:T(4,128)S(1)} %add_add_fusion), channel_id=1, source_target_pairs={{0,4},{1,5},{2,6},{3,7},{4,0},{5,1},{6,2},{7,3},{8,12},{9,13},{10,... | collective-permute-start | bytes 12296 | tf_op jit(solution)/shard_map/ppermute | solution.py:352
  154.2 5.4 %collective-permute-start.29 = (f32[4,256]{1,0:T(4,128)S(1)}, f32[4,256]{1,0:T(4,128)S(1)}, u32[]{:S(2)}, u32[]{:S(2)}) collective-permute-start(f32[4,256]{1,0:T(4,128)S(1)} %add.213), channel_id=1, source_target_pairs={{0,8},{1,9},{2,10},{3,11},{4,12},{5,13},{6,14},{7,15},{8,16},{9,17... | collective-permute-start | bytes 12296 | tf_op jit(solution)/shard_map/ppermute | solution.py:352
  154.2 5.4 %collective-permute-start.30 = (f32[4,256]{1,0:T(4,128)S(1)}, f32[4,256]{1,0:T(4,128)S(1)}, u32[]{:S(2)}, u32[]{:S(2)}) collective-permute-start(f32[4,256]{1,0:T(4,128)S(1)} %add.213), channel_id=1, source_target_pairs={{0,16},{1,17},{2,18},{3,19},{4,20},{5,21},{6,22},{7,23},{8,24},{9,... | collective-permute-start | bytes 12296 | tf_op jit(solution)/shard_map/ppermute | solution.py:352
  156.1 4.1 %collective-permute-start.31 = (f32[4,256]{1,0:T(4,128)S(1)}, f32[4,256]{1,0:T(4,128)S(1)}, u32[]{:S(2)}, u32[]{:S(2)}) collective-permute-start(f32[4,256]{1,0:T(4,128)S(1)} %add.213), channel_id=1, source_target_pairs={{0,24},{1,25},{2,26},{3,27},{4,28},{5,29},{6,30},{7,31},{8,0},{9,1... | collective-permute-start | bytes 12296 | tf_op jit(solution)/shard_map/ppermute | solution.py:352
  (11 other events, 95.2 us)
